TPU v7x, 32 devices: a whole 2x2x4 slice. The times are simulated.
32 devices in a mesh: space: 8 (over z, x), vel: 4 (over y, core).
Axes of the slice: x: 2, y: 2, z: 4, core: 2. Of those that a mesh axis runs over, the one named last changes fastest.
Arguments:
- dist: float32 [32, 48, 2304], P('space', 'vel'), may hold values from 0.4 to 18
- inflow: float32 [48, 2304], P('vel'), may hold values from 0.1 to 3
- neighbor: int32 [4, 32], P(None, 'space'), may hold values from 0 to 31, as said below
- face_kind: int32 [4, 32], P(None, 'space'), may hold values from 0 to 2, as said below
- member: int32 [32], P('space'), may hold values 0 or 1
- face_coef: float32 [4, 32], P(None, 'space'), may hold values from 0.02 to 0.12
- face_angles: float32 [2, 4, 32], P(None, None, 'space'), may hold values from -3.140625 to 3.140625
- dir_angles: float32 [2, 6], replicated, may hold values from -3.140625 to 3.140625
- dir_weights: float32 [6], replicated, may hold values from 0.2 to 0.8
- relax_step: float32 [32], P('space'), may hold values from 0.05 to 0.3
- pen_rate: float32 [32], P('space'), may hold values from 0.2 to 1
Outputs:
- new_dist: float32 [32, 48, 2304], P('space', 'vel')
Inputs may be any that keep to these rules, and one draw needn't show every extreme that they name: `neighbor`: each face's neighbour is another cell at most 4 cell numbers away, and that distance occurs. `face_kind`: 0 takes the neighbour cell, 1 the inflow state, 2 the cell itself.
All inputs are finite; a program needn't handle non-finite values. No bound on the sum of `member` on one device may be relied on, other than what follows from the above.
Results may differ from a plain program's by a relative error of at most 0.0003.
Values sent between devices are 32-bit elements; how exact they have to be, the bound alone decides.
A program may use at most 128 MiB of HBM per device.

v0:
```python
import math

import jax
import jax.numpy as jnp
import numpy as np
from jax import lax
from jax.experimental import pallas as pl
from jax.experimental.pallas import tpu as pltpu
from jax.sharding import PartitionSpec as P

NV = 48
LANES = 128
CHUNK = 8


HIGHEST_PRECISION = lax.Precision.HIGHEST


def extended(shard, sides, width):
    for axis, dim in sides:
        count, length = (lax.axis_size(axis), shard.shape[dim])
        up = [(i, (i + 1) % count) for i in range(count - 1)]
        down = [(j, i) for i, j in up]
        last = lax.slice_in_dim(shard, length - width, length, axis=dim)
        initial = lax.slice_in_dim(shard, 0, width, axis=dim)
        before = lax.ppermute(last, axis, up)
        after = lax.ppermute(initial, axis, down)
        shard = jnp.concatenate([before, shard, after], axis=dim)
    return shard


def velocity_grid(points):
    return (2.0 * jnp.arange(points, dtype=jnp.float32) + 1.0 - points) / points


def velocity_parts(first_rows, points, columns):
    column = jnp.arange(columns, dtype=jnp.int32)
    vel_y = ((2.0 * (column // points).astype(jnp.float32) + 1.0 - points) / points)[None, :]
    vel_z = ((2.0 * (column % points).astype(jnp.float32) + 1.0 - points) / points)[None, :]
    return (first_rows[:, None], vel_y, vel_z)


def moment_sums(values, vel_x, vel_y, vel_z):
    speed_sq = vel_x * vel_x + vel_y * vel_y + vel_z * vel_z
    return (
        jnp.sum(values, axis=(-2, -1)),
        jnp.sum(values * vel_x, axis=(-2, -1)),
        jnp.sum(values * vel_y, axis=(-2, -1)),
        jnp.sum(values * vel_z, axis=(-2, -1)),
        jnp.sum(values * speed_sq, axis=(-2, -1)),
    )


def maxwellian(totals, vel_x, vel_y, vel_z, points):
    particle_amount_local = totals[0][..., None, None]
    mean_flow_first = totals[1][..., None, None] / particle_amount_local
    mean_flow_second = totals[2][..., None, None] / particle_amount_local
    mean_flow_third = totals[3][..., None, None] / particle_amount_local
    motion_work_total = totals[4][..., None, None]
    heat_level = (
        motion_work_total / particle_amount_local
        - (
            mean_flow_first * mean_flow_first
            + mean_flow_second * mean_flow_second
            + mean_flow_third * mean_flow_third
        )
    ) / 3.0
    lattice_spacing = 2.0 / points
    scaling_divisor = (
        particle_amount_local * lattice_spacing**3 * (2.0 * math.pi * heat_level) ** (-1.5)
    )
    relative_motion_norm = (
        (vel_x - mean_flow_first) ** 2
        + (vel_y - mean_flow_second) ** 2
        + (vel_z - mean_flow_third) ** 2
    )
    return scaling_divisor * jnp.exp(-relative_motion_norm / (2.0 * heat_level))


def trig_tables(points):
    half = points // 2
    order = np.arange(points) % half
    is_sine = np.arange(points) >= half
    angle = 2.0 * np.pi * ((order[:, None] * np.arange(points)[None, :]) % points) / points
    cosine, sine = np.cos(angle), np.sin(angle)
    back = np.where(is_sine[:, None], sine, cosine)
    weight = np.where(order == 0, 1.0, 2.0)[:, None] / points
    even = weight * back
    odd = weight * np.where(is_sine[:, None], cosine, -sine)
    dead = (order == 0) & is_sine
    odd[order == 0] = 0.0
    even[dead] = 0.0
    return even, odd, back.T, order


def lane_block(matrix, copies):
    out = np.zeros((LANES, LANES))
    n = matrix.shape[0]
    for row, col in copies:
        out[row * n : (row + 1) * n, col * n : (col + 1) * n] = matrix
    return out


def dot3(a, b):
    return jnp.dot(a, b, precision=lax.Precision.HIGH, preferred_element_type=jnp.float32)


def gain_kernel(
    cube_ref, fz_ref, fyx_ref, iz_ref, iv_ref, freq_ref, lane_ref, dirs_ref, acc_ref,
    y00, y10, y01, y11, h1, h2, h3, h4, ta, tb, tab,
):
    n = NV
    chunks = n // CHUNK

    def forward_yz(i, carry):
        rows = pl.multiple_of(i * (CHUNK * n), CHUNK * n)
        z = dot3(cube_ref[pl.ds(rows, CHUNK * n), :], fz_ref[...])
        for u in range(CHUNK):
            out = dot3(fyx_ref[...], z[u * n : (u + 1) * n, :])
            here = pl.ds(rows + u * n, n)
            y00[here, :] = out[:n, :LANES]
            y10[here, :] = out[n:, :LANES]
            y01[here, :] = out[:n, LANES:]
            y11[here, :] = out[n:, LANES:]
        return carry

    lax.fori_loop(0, chunks, forward_yz, 0)

    def forward_x(i, carry):
        for u in range(CHUNK):
            q = i * CHUNK + u
            pick = pl.ds(q, n, stride=n)
            even = dot3(fyx_ref[:n, :], jnp.concatenate([y00[pick, :], y11[pick, :]], axis=1))
            odd = dot3(fyx_ref[n:, :], jnp.concatenate([y10[pick, :], y01[pick, :]], axis=1))
            g000, g011 = even[:, :LANES], even[:, LANES:]
            g110, g101 = odd[:, :LANES], odd[:, LANES:]
            here = pl.ds(pl.multiple_of(q * n, n), n)
            h1[here, :] = 0.25 * ((g000 - g110) - (g101 + g011))
            h2[here, :] = 0.25 * ((g000 - g110) + (g101 + g011))
            h3[here, :] = 0.25 * ((g000 + g110) - (g101 - g011))
            h4[here, :] = 0.25 * ((g000 + g110) + (g101 - g011))
        return carry

    lax.fori_loop(0, chunks, forward_x, 0)

    turn = 2.0 * math.pi / 8.0
    for pack in range(dirs_ref.shape[0]):
        e_x = dirs_ref[pack, 0:1, :]
        e_y = dirs_ref[pack, 1:2, :]
        e_z = dirs_ref[pack, 2:3, :]
        weight = dirs_ref[pack, 3:4, :]
        a = freq_ref[...] * e_x
        c = lane_ref[...] * e_z
        cos_a, sin_a = jnp.cos(a * turn), jnp.sin(a * turn)
        cos_c, sin_c = jnp.cos(c * turn), jnp.sin(c * turn)
        b_all = freq_ref[...] * e_y
        tab[0] = b_all
        tab[1] = jnp.cos(b_all * turn)
        tab[2] = jnp.sin(b_all * turn)

        def inverse_zx(i, carry):
            packed = []
            for u in range(CHUNK):
                q = i * CHUNK + u
                here = pl.ds(pl.multiple_of(q * n, n), n)
                b = tab[0, pl.ds(q, 1), :]
                cos_b = tab[1, pl.ds(q, 1), :]
                sin_b = tab[2, pl.ds(q, 1), :]
                f1, f2, f3, f4 = h1[here, :], h2[here, :], h3[here, :], h4[here, :]
                cc, ss = cos_a * cos_b, sin_a * sin_b
                sc, cs = sin_a * cos_b, cos_a * sin_b
                shifting = cos_c * ((cc - ss) * (f1 + f2) + (cc + ss) * (f3 + f4)) + sin_c * (
                    (sc + cs) * (f2 - f1) + (sc - cs) * (f4 - f3)
                )
                up, um = a + b, a - b
                smoothing = 0.0
                for kappa, part in ((up + c, f1), (up - c, f2), (um + c, f3), (um - c, f4)):
                    smoothing += jnp.exp(kappa * kappa * (-8.0 / (NV * NV))) * part
                packed.append(jnp.concatenate([shifting, weight * smoothing], axis=1))
            z = dot3(jnp.concatenate(packed, axis=0), iz_ref[...])
            for u in range(CHUNK):
                out = dot3(iv_ref[...], z[u * n : (u + 1) * n, :])
                here = pl.ds(pl.multiple_of((i * CHUNK + u) * n, n), n)
                ta[here, :] = out[:, :LANES]
                tb[here, :] = out[:, LANES:]
            return carry

        lax.fori_loop(0, chunks, inverse_zx, 0)

        def inverse_y(i, carry):
            for u in range(CHUNK):
                q = i * CHUNK + u
                pick = pl.ds(q, n, stride=n)
                out = dot3(iv_ref[...], jnp.concatenate([ta[pick, :], tb[pick, :]], axis=1))
                here = pl.ds(pl.multiple_of(q * n, n), n)
                term = out[:, LANES:] * (out[:, :LANES] - cube_ref[here, :])
                if pack == 0:
                    acc_ref[here, :] = term
                else:
                    acc_ref[here, :] += term
            return carry

        lax.fori_loop(0, chunks, inverse_y, 0)


def collision_gain(cube, dir_angles, dir_weights):
    even, odd, back, order = trig_tables(NV)
    count = dir_angles.shape[1]
    packs = count // 2
    dup = ((0, 0), (0, 1))
    f_z = np.concatenate([lane_block(even.T, dup), lane_block(odd.T, dup)], axis=1)
    diag = lane_block(back.T, ((0, 0), (1, 1)))
    i_z = np.kron(np.eye(2), diag)
    f_yx = np.concatenate([even, odd], axis=0)
    lane = np.zeros((1, LANES))
    lane[0, : 2 * NV] = np.tile(order, 2)
    freq = np.tile(order[:, None], (1, LANES))
    azimuth, elevation = dir_angles[0], dir_angles[1]
    dirs = jnp.stack(
        [
            jnp.cos(azimuth) * jnp.cos(elevation),
            jnp.sin(azimuth) * jnp.cos(elevation),
            jnp.sin(elevation),
            dir_weights,
        ]
    )
    dirs = jnp.repeat(dirs, NV, axis=1).reshape(4, packs, 2 * NV).transpose(1, 0, 2)
    dirs = jnp.pad(dirs, ((0, 0), (0, 0), (0, LANES - 2 * NV)))
    flat = cube.reshape(NV * NV, NV)
    doubled = jnp.concatenate(
        [flat, flat, jnp.zeros((NV * NV, LANES - 2 * NV), jnp.float32)], axis=1
    )
    table = lambda t: jnp.asarray(t, jnp.float32)
    big = pltpu.VMEM((NV * NV, LANES), jnp.float32)
    acc = pl.pallas_call(
        gain_kernel,
        out_shape=jax.ShapeDtypeStruct((NV * NV, LANES), jnp.float32),
        in_specs=[pl.BlockSpec(memory_space=pltpu.VMEM)] * 8,
        out_specs=pl.BlockSpec(memory_space=pltpu.VMEM),
        scratch_shapes=[big] * 10 + [pltpu.VMEM((3, NV, LANES), jnp.float32)],
        compiler_params=pltpu.CompilerParams(vmem_limit_bytes=40 * 1024 * 1024),
        cost_estimate=pl.CostEstimate(
            flops=2 * 10**9, bytes_accessed=4 * 10**6, transcendentals=2 * 10**6
        ),
    )(doubled, table(f_z), table(f_yx), table(i_z), table(back), table(freq), table(lane), dirs)
    return (acc[:, :NV] + acc[:, NV : 2 * NV]).reshape(NV, NV * NV)


def body(
    dist,
    inflow,
    neighbor,
    face_kind,
    member,
    face_coef,
    face_angles,
    dir_angles,
    dir_weights,
    relax_step,
    pen_rate,
):
    cells_dev, slab_rows, columns = dist.shape
    face_count = neighbor.shape[0]
    groups = lax.axis_size("vel")
    vel_index = lax.axis_index("vel")
    grid_points = velocity_grid(NV)
    slab_x = lax.dynamic_slice_in_dim(grid_points, vel_index * slab_rows, slab_rows)
    vel_x, vel_y, vel_z = velocity_parts(slab_x, NV, columns)
    padded = extended(dist, (("space", 0),), cells_dev)
    first_cell = lax.axis_index("space") * cells_dev - cells_dev
    local_slot = neighbor - first_cell
    onehot = (
        local_slot[:, :, None] == jnp.arange(3 * cells_dev, dtype=jnp.int32)[None, None, :]
    ).astype(jnp.float32)
    nearby = jnp.dot(
        onehot.reshape(face_count * cells_dev, 3 * cells_dev),
        padded.reshape(3 * cells_dev, slab_rows * columns),
        precision=HIGHEST_PRECISION,
    ).reshape(face_count, cells_dev, slab_rows, columns)
    face_type = face_kind[:, :, None, None]
    upwind = jnp.where(
        face_type == 0, nearby, jnp.where(face_type == 1, inflow[None, None], dist[None])
    )
    azimuth = face_angles[0][:, :, None, None]
    elevation = face_angles[1][:, :, None, None]
    normal_dot = (
        jnp.cos(azimuth) * jnp.cos(elevation) * vel_x[None, None]
        + jnp.sin(azimuth) * jnp.cos(elevation) * vel_y[None, None]
        + jnp.sin(elevation) * vel_z[None, None]
    )
    coefficient = face_coef[:, :, None, None]
    face_flux = jnp.sum(
        coefficient
        * (jnp.maximum(normal_dot, 0.0) * dist[None] + jnp.minimum(normal_dot, 0.0) * upwind),
        axis=0,
    )
    per_device = cells_dev // groups
    blocks = dist.reshape(groups, per_device, slab_rows, columns)
    whole_cells = lax.all_to_all(blocks, "vel", split_axis=0, concat_axis=2, tiled=True).reshape(
        per_device, NV, columns
    )
    first_slot = vel_index * per_device
    relax_mine = lax.dynamic_slice_in_dim(relax_step, first_slot, per_device)
    pen_mine = lax.dynamic_slice_in_dim(pen_rate, first_slot, per_device)
    full_x, full_y, full_z = velocity_parts(grid_points, NV, columns)

    def one_cell(packed):
        own_cell, relax_one, pen_one = packed
        maxwell = maxwellian(
            moment_sums(own_cell, full_x, full_y, full_z), full_x, full_y, full_z, NV
        )
        gain_term = collision_gain(own_cell.reshape(NV, NV, NV), dir_angles, dir_weights)
        return relax_one * (gain_term - pen_one * (own_cell - maxwell))

    increments = jnp.stack(
        [one_cell((whole_cells[i], relax_mine[i], pen_mine[i])) for i in range(per_device)]
    )
    increment = lax.all_to_all(
        increments.reshape(1, per_device, NV, columns),
        "vel",
        split_axis=2,
        concat_axis=0,
        tiled=True,
    )
    increment = increment.reshape(cells_dev, slab_rows, columns)
    advanced = dist - face_flux + increment
    return jnp.where(member[:, None, None] == 1, advanced, dist)


def solution(mesh):
    placed = (
        P("space", "vel", None),
        P("vel", None),
        P(None, "space"),
        P(None, "space"),
        P("space"),
        P(None, "space"),
        P(None, None, "space"),
        P(),
        P(),
        P("space"),
        P("space"),
    )
    return jax.shard_map(
        body, mesh=mesh, in_specs=placed, out_specs=P("space", "vel", None), check_vma=False
    )
```

profile of v0, /device:TPU:0, one launch (start us, length us, event | category | flops | bytes accessed | tf_op | source)
XLA Modules:
  0.0 87.2 jit_solution(12041081682931457313)
XLA Ops:
  0.0 0.0 copy-start.8
  0.0 0.0 copy-start.16
  0.0 0.0 copy-start.9
  0.0 1.4 %collective-permute-start.1 = (f32[4,12,2304]{2,0,1:T(4,128)}, f32[4,12,2304]{2,0,1:T(4,128)S(1)}, u32[]{:S(2)}, u32[]{:S(2)}) collective-permute-start(f32[4,12,2304]{2,0,1:T(4,128)} %param.17), channel_id=1, source_target_pairs={{4,0},{8,4},{12,8},{16,12},{20,16},{24,20},{28,24},{5,1},{9,5},{13... | collective-permute-start | bytes 1327112 | tf_op jit(solution)/shard_map/ppermute | solution.py:27
  1.5 6.3 %collective-permute-start = (f32[4,12,2304]{2,0,1:T(4,128)}, f32[4,12,2304]{2,0,1:T(4,128)}, u32[]{:S(2)}, u32[]{:S(2)}) collective-permute-start(f32[4,12,2304]{2,0,1:T(4,128)} %param.17), channel_id=1, source_target_pairs={{0,4},{4,8},{8,12},{12,16},{16,20},{20,24},{24,28},{1,5},{5,9},{9,... | collective-permute-start | bytes 1327112 | tf_op jit(solution)/shard_map/ppermute | solution.py:26
  7.7 2.2 %copy.44 = f32[4,1,12,2304]{3,1,2,0:T(1,128)} copy(f32[4,1,12,2304]{3,0,2,1:T(4,128)} %bitcast.34) | data formatting | bytes 884736 | tf_op jit(solution)/shard_map/reshape | solution.py:298
  10.0 3.5 %all-to-all-start = ((f32[4,1,12,2304]{3,1,2,0:T(1,128)}), f32[4,1,12,2304]{3,1,2,0:T(1,128)S(1)}, u32[]{:S(2)}, u32[]{:S(2)}) async-start(f32[4,1,12,2304]{3,1,2,0:T(1,128)} %copy.44), calls=%async_computation | async-start | bytes 884736 | tf_op jit(solution)/shard_map/all_to_all | solution.py:299
  13.5 0.0 copy-done.10
  13.5 0.1 cosine_multiply_fusion
  13.6 0.1 broadcast_in_dim.44
  13.7 0.1 reshape_reshape.3
  13.8 0.7 dynamic_slice.11
  14.4 0.6 dynamic_slice.10
  15.2 0.1 pad.11.clone
  15.2 0.1 broadcast_multiply_fusion
  15.3 0.1 broadcast_multiply_fusion.1
  15.4 0.1 dynamic_slice.9
  15.5 0.1 broadcast_multiply_fusion.2
  15.6 5.8 %all-to-all-done = f32[4,1,12,2304]{3,1,2,0:T(1,128)S(1)} async-done(((f32[4,1,12,2304]{3,1,2,0:T(1,128)}), f32[4,1,12,2304]{3,1,2,0:T(1,128)S(1)}, u32[]{:S(2)}, u32[]{:S(2)}) %all-to-all-start) | async-done | bytes 442400 | tf_op jit(solution)/shard_map/all_to_all | solution.py:299
  21.4 3.6 %multiply_reduce_fusion = (f32[]{:T(128)}, f32[]{:T(128)}, f32[]{:T(128)}, f32[]{:T(128)}, f32[]{:T(128)}, /*index=5*/f32[4,12,2304]{2,1,0:T(8,128)S(1)}) fusion(f32[4,1,12,2304]{3,1,2,0:T(1,128)S(1)} %all-to-all-done, f32[2304]{0:T(1024)S(1)} %get-tuple-element.20, f32[2304]{0:T(1024)S(1)} %get-tuple-element.19, f32[4,12]{1,0:T(4,128)S(1)} %get-tuple-element.23, ...), kind=kLoop, calls=%fused_computation.16 | loop fusion | flops 1216507 | bytes 922004 | tf_op jit(solution)/shard_map/reduce_sum | solution.py:49
  28.7 0.0 copy-start
  28.7 0.0 copy-start.1
  28.7 0.0 copy-start.2
  28.8 0.0 copy-start.3
  28.8 0.0 copy-start.4
  28.8 0.0 copy-start.5
  28.8 0.7 reshape_reshape_squeeze_reshape.3
  29.5 0.4 maximum_maximum_fusion.cube_ref
  30.0 35.4 %shard_map.163 = f32[2304,128]{1,0:T(8,128)S(1)} custom-call(f32[2304,128]{1,0:T(8,128)S(1)} %maximum_maximum_fusion.cube_ref, f32[128,256]{1,0:T(8,128)S(1)} %copy-done.1, f32[96,48]{1,0:T(8,128)S(1)} %copy-done.2, f32[256,256]{1,0:T(8,128)S(1)} %copy-done, f32[48,48]{1,0:T(8,128)S(1)} %copy-done.3, f32[48,128]{1,0:T(8,128)S(1)} %copy-done.4, ...), custom_call_target="tpu_custom_call" | custom-call | flops 2000000000 | bytes 4000000 | tf_op jit(solution)/shard_map/pallas_call | solution.py:235
  65.4 0.4 slice_add_fusion
  65.8 0.5 reshape.375
  68.3 1.5 %fusion.11 = f32[1,1,48,2304]{3,2,1,0:T(8,128)S(1)} fusion(f32[1,1,48,2304]{3,2,1,0:T(8,128)S(1)} %reshape.375, f32[1,1,48,2304]{3,0,2,1:T(1,128)S(1)} %bitcast.35, f32[]{:T(128)S(6)} %mul.361, f32[]{:T(128)S(6)} %mul.360, f32[2304]{0:T(1024)S(1)} %subtract_multiply_fusion, f32[2304]{0:T(1024)S(1)} %subtract_multiply_fusion.1, ...), kind=kLoop, calls=%fused_computation.15 | loop fusion | flops 995328 | bytes 1345744 | tf_op jit(solution)/shard_map/mul | solution.py:313
  69.8 1.2 %copy.47 = f32[1,1,48,2304]{3,1,0,2:T(1,128)} copy(f32[1,1,48,2304]{3,2,1,0:T(8,128)S(1)} %fusion.11) | data formatting | bytes 884736 | tf_op jit(solution)/shard_map/mul | solution.py:313
  71.0 3.6 %all-to-all-start.1 = ((f32[1,1,48,2304]{3,1,0,2:T(1,128)}), f32[1,1,48,2304]{3,1,0,2:T(1,128)S(1)}, u32[]{:S(2)}, u32[]{:S(2)}) async-start(f32[1,1,48,2304]{3,1,0,2:T(1,128)} %copy.47), calls=%async_computation.1 | async-start | bytes 884736 | tf_op jit(solution)/shard_map/all_to_all | solution.py:318
  74.6 0.0 collective-permute-done.1
  74.6 0.0 collective-permute-done
  74.6 0.0 copy-done.6
  74.7 1.3 %pad_maximum_fusion = f32[12,12,2304]{2,0,1:T(8,128)S(1)} fusion(f32[4,12,2304]{2,0,1:T(4,128)S(1)} %collective-permute-done.1, f32[4,12,2304]{2,0,1:T(4,128)S(1)} %copy-done.6, f32[4,12,2304]{2,0,1:T(4,128)} %collective-permute-done), kind=kLoop, calls=%fused_computation.4 | loop fusion | flops 663552 | bytes 2654208 | tf_op jit(solution)/shard_map/concatenate | solution.py:28
  76.0 0.8 copy.42
  76.8 0.2 pad.15
  77.0 1.0 %copy.51 = f32[2,8,12,2304]{3,1,2,0:T(8,128)S(1)} copy(f32[2,8,12,2304]{3,2,1,0:T(8,128)S(1)} %bitcast.32) | data formatting | bytes 3538944
  78.0 0.0 copy-start.12
  78.0 0.0 copy-start.13
  78.0 1.7 %dot_general.8 = f32[12,2304,12]{1,0,2:T(8,128)} reshape(f32[27648,12]{0,1:T(8,128)S(1)} %bitcast.33) | data formatting | bytes 2654208 | tf_op jit(solution)/shard_map/dot_general | solution.py:275
  79.8 5.2 %fusion.5 = f32[4,12,2304]{2,0,1:T(4,128)S(1)} fusion(f32[12,2304,12]{1,0,2:T(8,128)} %dot_general.8, f32[12,2304]{1,0:T(8,128)S(1)} %copy-done.12, f32[4,12,2304]{2,0,1:T(4,128)S(1)} %copy-done.6, f32[4,4,2304]{2,1,0:T(4,128)S(1)} %broadcast_multiply_fusion, f32[4,4,2304]{2,1,0:T(4,128)S(1)} %broadcast_multiply_fusion.1, ...), kind=kOutput, calls=%fused_computation.7 | convolution fusion | flops 68456640 | bytes 2618272 | tf_op jit(solution)/shard_map/dot_general | solution.py:275
  84.9 0.0 all-to-all-done.1
  84.9 1.0 %reduce.6 = f32[48,2304]{1,0:T(8,128)S(1)} reduce(f32[1,1,48,2304]{3,1,0,2:T(1,128)S(1)} %all-to-all-done.1, f32[]{:T(128)} %constant.117), dimensions={0,1}, to_apply=%all_to_all.5.reduce_sub_computation | reduce | bytes 884740 | tf_op jit(solution)/shard_map/all_to_all | solution.py:318
  86.0 1.2 %fusion.8 = f32[4,12,2304]{2,0,1:T(4,128)} fusion(f32[4,12,2304]{2,0,1:T(4,128)S(1)} %copy-done.6, f32[4,12,2304]{2,1,0:T(8,128)S(1)} %reshape.376, f32[4,12,2304]{2,0,1:T(4,128)S(1)} %fusion.5, pred[4]{0:T(512)(128)(4,1)S(1)} %broadcast_compare_fusion.2), kind=kLoop, calls=%fused_computation.11 | loop fusion | flops 331776 | bytes 1769476 | tf_op jit(solution)/shard_map/jit(_where)/select_n | solution.py:327
  (37 shorter events, 0.3 us)
Async XLA Ops:
  0.0 13.5 %copy-start.10 = (f32[2,6]{1,0:T(2,128)S(1)}, f32[2,6]{1,0:T(2,128)}, u32[]{:S(2)}) copy-start(f32[2,6]{1,0:T(2,128)} %param.24) | copy-start | bytes 148
  0.0 13.6 %copy-start.11 = (f32[6]{0:T(128)S(1)}, f32[6]{0:T(128)}, u32[]{:S(2)}) copy-start(f32[6]{0:T(128)} %param.25) | copy-start | bytes 76
  0.0 13.7 %copy-start.14 = (f32[4]{0:T(128)S(1)}, f32[4]{0:T(128)}, u32[]{:S(2)}) copy-start(f32[4]{0:T(128)} %param.27) | copy-start | bytes 52
  0.0 14.4 %copy-start.15 = (f32[4]{0:T(128)S(1)}, f32[4]{0:T(128)}, u32[]{:S(2)}) copy-start(f32[4]{0:T(128)} %param.26) | copy-start | bytes 52
  0.0 15.0 %copy-start.7 = (f32[2,4,4]{2,1,0:T(4,128)S(1)}, f32[2,4,4]{2,1,0:T(4,128)}, u32[]{:S(2)}) copy-start(f32[2,4,4]{2,1,0:T(4,128)} %param.23) | copy-start | bytes 388
  0.0 15.1 %copy-start.8 = (s32[4,4]{1,0:T(4,128)S(1)}, s32[4,4]{1,0:T(4,128)}, u32[]{:S(2)}) copy-start(s32[4,4]{1,0:T(4,128)} %param.20) | copy-start | bytes 196
  0.0 15.1 %copy-start.16 = (s32[4]{0:T(128)S(1)}, s32[4]{0:T(128)}, u32[]{:S(2)}) copy-start(s32[4]{0:T(128)} %param.21) | copy-start | bytes 52
  0.0 15.5 %copy-start.9 = (s32[4,4]{1,0:T(4,128)S(1)}, s32[4,4]{1,0:T(4,128)}, u32[]{:S(2)}) copy-start(s32[4,4]{1,0:T(4,128)} %param.19) | copy-start | bytes 196
  0.0 74.6 %collective-permute-start.1 = (f32[4,12,2304]{2,0,1:T(4,128)}, f32[4,12,2304]{2,0,1:T(4,128)S(1)}, u32[]{:S(2)}, u32[]{:S(2)}) collective-permute-start(f32[4,12,2304]{2,0,1:T(4,128)} %param.17), channel_id=1, source_target_pairs={{4,0},{8,4},{12,8},{16,12},{20,16},{24,20},{28,24},{5,1},{9,5},{13... | collective-permute-start | bytes 1327112 | tf_op jit(solution)/shard_map/ppermute | solution.py:27
  1.5 73.2 %collective-permute-start = (f32[4,12,2304]{2,0,1:T(4,128)}, f32[4,12,2304]{2,0,1:T(4,128)}, u32[]{:S(2)}, u32[]{:S(2)}) collective-permute-start(f32[4,12,2304]{2,0,1:T(4,128)} %param.17), channel_id=1, source_target_pairs={{0,4},{4,8},{8,12},{12,16},{16,20},{20,24},{24,28},{1,5},{5,9},{9,... | collective-permute-start | bytes 1327112 | tf_op jit(solution)/shard_map/ppermute | solution.py:26
  10.0 11.4 %all-to-all-start = ((f32[4,1,12,2304]{3,1,2,0:T(1,128)}), f32[4,1,12,2304]{3,1,2,0:T(1,128)S(1)}, u32[]{:S(2)}, u32[]{:S(2)}) async-start(f32[4,1,12,2304]{3,1,2,0:T(1,128)} %copy.44), calls=%async_computation | async-start | bytes 884736 | tf_op jit(solution)/shard_map/all_to_all | solution.py:299
  28.7 1.2 %copy-start = (f32[256,256]{1,0:T(8,128)S(1)}, f32[256,256]{1,0:T(8,128)}, u32[]{:S(2)}) copy-start(f32[256,256]{1,0:T(8,128)} %constant.100.clone.iz_ref) | copy-start | bytes 786436
  28.7 1.2 %copy-start.1 = (f32[128,256]{1,0:T(8,128)S(1)}, f32[128,256]{1,0:T(8,128)}, u32[]{:S(2)}) copy-start(f32[128,256]{1,0:T(8,128)} %constant.98.clone.fz_ref) | copy-start | bytes 393220
  28.7 1.2 %copy-start.2 = (f32[96,48]{1,0:T(8,128)S(1)}, f32[96,48]{1,0:T(8,128)}, u32[]{:S(2)}) copy-start(f32[96,48]{1,0:T(8,128)} %constant.99.clone.fyx_ref) | copy-start | bytes 55300
  28.8 1.2 %copy-start.3 = (f32[48,48]{1,0:T(8,128)S(1)}, f32[48,48]{1,0:T(8,128)}, u32[]{:S(2)}) copy-start(f32[48,48]{1,0:T(8,128)} %constant.101.clone.iv_ref) | copy-start | bytes 27652
  28.8 1.2 %copy-start.4 = (f32[48,128]{1,0:T(8,128)S(1)}, f32[48,128]{1,0:T(8,128)}, u32[]{:S(2)}) copy-start(f32[48,128]{1,0:T(8,128)} %constant.102.clone.freq_ref) | copy-start | bytes 73732
  28.8 1.2 %copy-start.5 = (f32[1,128]{1,0:T(1,128)S(1)}, f32[1,128]{1,0:T(1,128)}, u32[]{:S(2)}) copy-start(f32[1,128]{1,0:T(1,128)} %constant.103.clone.lane_ref) | copy-start | bytes 1540
  66.3 8.3 %copy-start.6 = (f32[4,12,2304]{2,0,1:T(4,128)S(1)}, f32[4,12,2304]{2,0,1:T(4,128)}, u32[]{:S(2)}) copy-start(f32[4,12,2304]{2,0,1:T(4,128)} %param.17) | copy-start | bytes 1327108
  71.0 14.0 %all-to-all-start.1 = ((f32[1,1,48,2304]{3,1,0,2:T(1,128)}), f32[1,1,48,2304]{3,1,0,2:T(1,128)S(1)}, u32[]{:S(2)}, u32[]{:S(2)}) async-start(f32[1,1,48,2304]{3,1,0,2:T(1,128)} %copy.47), calls=%async_computation.1 | async-start | bytes 884736 | tf_op jit(solution)/shard_map/all_to_all | solution.py:318
  78.0 1.8 %copy-start.12 = (f32[12,2304]{1,0:T(8,128)S(1)}, f32[12,2304]{1,0:T(8,128)}, u32[]{:S(2)}) copy-start(f32[12,2304]{1,0:T(8,128)} %param.18) | copy-start | bytes 331780
  78.0 1.8 %copy-start.13 = (f32[4,4]{1,0:T(4,128)S(1)}, f32[4,4]{1,0:T(4,128)}, u32[]{:S(2)}) copy-start(f32[4,4]{1,0:T(4,128)} %param.22) | copy-start | bytes 196
where the time goes:
time: 87.7 us; the launch traced here: 87.2 us
  Pallas kernels  35.4 us (40%)
  starting transfers between devices  14.8 us (17%)
  local copies, waits for them, and re-layouts  10.2 us (12%)
  other arithmetic  9.8 us (11%)
  between operations  6.07 us (7%)
  waiting for transfers between devices  5.79 us (7%)
  matrix products  5.15 us (6%)
    pallas_call x1, Pallas kernels, collision_gain(): pl.pallas_call(gain_kernel, out_shape=jax.ShapeDtypeStruct((NV * NV, LANE...  35.4 us
    ppermute x1, starting transfers between devices, extended(): before = lax.ppermute(last, axis, up)  6.26 us
    all_to_all x1, waiting for transfers between devices, body(): lax.all_to_all(blocks, 'vel', split_axis=0, concat_axis=2, tiled=True)  5.78 us
    dot_general x1, matrix products, body(): jnp.dot(onehot.reshape(face_count * cells_dev, 3 * cells_dev), padded.res...  5.15 us
    all_to_all x1, starting transfers between devices, body(): lax.all_to_all(increments.reshape(1, per_device, NV, columns), 'vel', spl...  3.64 us
    reduce_sum x1, other arithmetic, moment_sums(): jnp.sum(values * vel_z, axis=(-2, -1))  3.59 us
    all_to_all x1, starting transfers between devices, body(): lax.all_to_all(blocks, 'vel', split_axis=0, concat_axis=2, tiled=True)  3.46 us
    reshape x1, local copies, waits for them, and re-layouts, body(): blocks = dist.reshape(groups, per_device, slab_rows, columns)  2.23 us
  transfers between devices with their start and end apart: 4, of which 1 were waited for; matrix products, arithmetic and copies ran while one was open for 26% of the time, Pallas kernels for 41%

commit v1 on v0

v1 whole, which is shorter than its diff:
```python
import math

import jax
import jax.numpy as jnp
import numpy as np
from jax import lax
from jax.experimental import pallas as pl
from jax.experimental.pallas import tpu as pltpu
from jax.sharding import PartitionSpec as P

NV = 48
LANES = 128
CHUNK = 8


def neighbours(shard, axis):
    count = lax.axis_size(axis)
    up = [(i, i + 1) for i in range(count - 1)]
    down = [(j, i) for i, j in up]
    return lax.ppermute(shard, axis, up), lax.ppermute(shard, axis, down)


def velocity_grid(points):
    return (2.0 * jnp.arange(points, dtype=jnp.float32) + 1.0 - points) / points


def trig_tables(points):
    half = points // 2
    order = np.arange(points) % half
    is_sine = np.arange(points) >= half
    angle = 2.0 * np.pi * ((order[:, None] * np.arange(points)[None, :]) % points) / points
    cosine, sine = np.cos(angle), np.sin(angle)
    back = np.where(is_sine[:, None], sine, cosine)
    weight = np.where(order == 0, 1.0, 2.0)[:, None] / points
    even = weight * back
    odd = weight * np.where(is_sine[:, None], cosine, -sine)
    dead = (order == 0) & is_sine
    odd[order == 0] = 0.0
    even[dead] = 0.0
    return even, odd, back.T, order


def lane_block(matrix, copies):
    out = np.zeros((LANES, LANES))
    n = matrix.shape[0]
    for row, col in copies:
        out[row * n : (row + 1) * n, col * n : (col + 1) * n] = matrix
    return out


def dot3(a, b):
    return jnp.dot(a, b, precision=lax.Precision.HIGH, preferred_element_type=jnp.float32)


def gain_kernel(
    rates_ref, cube_ref, fz_ref, fyx_ref, iz_ref, iv_ref, freq_ref, lane_ref, vel_ref, dirs_ref,
    inc_ref, acc_ref, y00, y10, y01, y11, h1, h2, h3, h4, ta, tb, tab,
):
    n = NV
    chunks = n // CHUNK
    packs = dirs_ref.shape[0]
    vel_y, vel_z, first_copy = vel_ref[0], vel_ref[1], vel_ref[2]

    def moments(q, sums):
        slab = cube_ref[pl.ds(pl.multiple_of(q * n, n), n), :]
        vel_x = (2.0 * q.astype(jnp.float32) + 1.0 - n) / n
        return sums[0] + slab, sums[1] + vel_x * slab, sums[2] + (vel_x * vel_x) * slab

    zero = jnp.zeros((n, LANES), jnp.float32)
    plain, along, squared = lax.fori_loop(0, n, moments, (zero, zero, zero), unroll=4)

    def whole(values):
        return jnp.sum(values * first_copy, keepdims=True)

    density = whole(plain)
    flow_x = whole(along) / density
    flow_y = whole(plain * vel_y) / density
    flow_z = whole(plain * vel_z) / density
    energy = whole(squared + plain * (vel_y * vel_y + vel_z * vel_z))
    heat = (energy / density - (flow_x * flow_x + flow_y * flow_y + flow_z * flow_z)) / 3.0
    wide = 2.0 * math.pi * heat
    peak = density * (2.0 / n) ** 3 / (wide * jnp.sqrt(wide))
    inverse_heat = 1.0 / (2.0 * heat)
    across = (vel_y[:, :n] - flow_y) ** 2 + (vel_z[:, :n] - flow_z) ** 2

    def forward_yz(i, carry):
        rows = pl.multiple_of(i * (CHUNK * n), CHUNK * n)
        z = dot3(cube_ref[pl.ds(rows, CHUNK * n), :], fz_ref[...])
        for u in range(CHUNK):
            out = dot3(fyx_ref[...], z[u * n : (u + 1) * n, :])
            here = pl.ds(rows + u * n, n)
            y00[here, :] = out[:n, :LANES]
            y10[here, :] = out[n:, :LANES]
            y01[here, :] = out[:n, LANES:]
            y11[here, :] = out[n:, LANES:]
        return carry

    lax.fori_loop(0, chunks, forward_yz, 0)

    def forward_x(i, carry):
        for u in range(CHUNK):
            q = i * CHUNK + u
            pick = pl.ds(q, n, stride=n)
            even = dot3(fyx_ref[:n, :], jnp.concatenate([y00[pick, :], y11[pick, :]], axis=1))
            odd = dot3(fyx_ref[n:, :], jnp.concatenate([y10[pick, :], y01[pick, :]], axis=1))
            g000, g011 = even[:, :LANES], even[:, LANES:]
            g110, g101 = odd[:, :LANES], odd[:, LANES:]
            here = pl.ds(pl.multiple_of(q * n, n), n)
            h1[here, :] = 0.25 * ((g000 - g110) - (g101 + g011))
            h2[here, :] = 0.25 * ((g000 - g110) + (g101 + g011))
            h3[here, :] = 0.25 * ((g000 + g110) - (g101 - g011))
            h4[here, :] = 0.25 * ((g000 + g110) + (g101 - g011))
        return carry

    lax.fori_loop(0, chunks, forward_x, 0)

    turn = 2.0 * math.pi / 8.0
    for pack in range(packs):
        azimuth = dirs_ref[pack, 0:1, :]
        elevation = dirs_ref[pack, 1:2, :]
        weight = dirs_ref[pack, 2:3, :]
        e_x = jnp.cos(azimuth) * jnp.cos(elevation)
        e_y = jnp.sin(azimuth) * jnp.cos(elevation)
        e_z = jnp.sin(elevation)
        a = freq_ref[...] * e_x
        c = lane_ref[...] * e_z
        cos_a, sin_a = jnp.cos(a * turn), jnp.sin(a * turn)
        cos_c, sin_c = jnp.cos(c * turn), jnp.sin(c * turn)
        b_all = freq_ref[...] * e_y
        tab[0] = b_all
        tab[1] = jnp.cos(b_all * turn)
        tab[2] = jnp.sin(b_all * turn)

        def inverse_zx(i, carry):
            packed = []
            for u in range(CHUNK):
                q = i * CHUNK + u
                here = pl.ds(pl.multiple_of(q * n, n), n)
                b = tab[0, pl.ds(q, 1), :]
                cos_b = tab[1, pl.ds(q, 1), :]
                sin_b = tab[2, pl.ds(q, 1), :]
                f1, f2, f3, f4 = h1[here, :], h2[here, :], h3[here, :], h4[here, :]
                cc, ss = cos_a * cos_b, sin_a * sin_b
                sc, cs = sin_a * cos_b, cos_a * sin_b
                shifting = cos_c * ((cc - ss) * (f1 + f2) + (cc + ss) * (f3 + f4)) + sin_c * (
                    (sc + cs) * (f2 - f1) + (sc - cs) * (f4 - f3)
                )
                up, um = a + b, a - b
                smoothing = 0.0
                for kappa, part in ((up + c, f1), (up - c, f2), (um + c, f3), (um - c, f4)):
                    smoothing += jnp.exp(kappa * kappa * (-8.0 / (NV * NV))) * part
                packed.append(jnp.concatenate([shifting, weight * smoothing], axis=1))
            z = dot3(jnp.concatenate(packed, axis=0), iz_ref[...])
            for u in range(CHUNK):
                out = dot3(iv_ref[...], z[u * n : (u + 1) * n, :])
                here = pl.ds(pl.multiple_of((i * CHUNK + u) * n, n), n)
                ta[here, :] = out[:, :LANES]
                tb[here, :] = out[:, LANES:]
            return carry

        lax.fori_loop(0, chunks, inverse_zx, 0)

        def inverse_y(i, carry):
            for u in range(CHUNK):
                q = i * CHUNK + u
                pick = pl.ds(q, n, stride=n)
                out = dot3(iv_ref[...], jnp.concatenate([ta[pick, :], tb[pick, :]], axis=1))
                here = pl.ds(pl.multiple_of(q * n, n), n)
                term = out[:, LANES:] * (out[:, :LANES] - cube_ref[here, :])
                if pack == 0:
                    acc_ref[here, :] = term
                elif pack < packs - 1:
                    acc_ref[here, :] += term
                else:
                    total = acc_ref[here, :] + term
                    vel_x = (2.0 * q.astype(jnp.float32) + 1.0 - n) / n
                    apart = (vel_x - flow_x) ** 2 + across
                    maxwell = peak * jnp.exp(-(apart * inverse_heat))
                    drift = cube_ref[here, :n] - maxwell
                    inc_ref[here, :] = rates_ref[0] * (
                        total[:, :n] + total[:, n : 2 * n] - rates_ref[1] * drift
                    )
            return carry

        lax.fori_loop(0, chunks, inverse_y, 0)


def collision_step(cube, rates, dir_angles, dir_weights):
    even, odd, back, order = trig_tables(NV)
    count = dir_angles.shape[1]
    packs = count // 2
    dup = ((0, 0), (0, 1))
    f_z = np.concatenate([lane_block(even.T, dup), lane_block(odd.T, dup)], axis=1)
    diag = lane_block(back.T, ((0, 0), (1, 1)))
    i_z = np.kron(np.eye(2), diag)
    f_yx = np.concatenate([even, odd], axis=0)
    lane = np.zeros((1, LANES))
    lane[0, : 2 * NV] = np.tile(order, 2)
    freq = np.tile(order[:, None], (1, LANES))
    dirs = jnp.concatenate([dir_angles, dir_weights[None]], axis=0)
    dirs = jnp.repeat(dirs, NV, axis=1).reshape(3, packs, 2 * NV).transpose(1, 0, 2)
    dirs = jnp.pad(dirs, ((0, 0), (0, 0), (0, LANES - 2 * NV)))
    speed = (2.0 * np.arange(NV) + 1.0 - NV) / NV
    inside = np.arange(LANES) < NV
    vel = np.zeros((3, NV, LANES))
    vel[0] = speed[:, None]
    vel[1, :, :NV] = speed[None, :]
    vel[2] = inside[None, :]
    flat = cube.reshape(NV * NV, NV)
    doubled = jnp.concatenate(
        [flat, flat, jnp.zeros((NV * NV, LANES - 2 * NV), jnp.float32)], axis=1
    )
    table = lambda t: jnp.asarray(t, jnp.float32)
    big = pltpu.VMEM((NV * NV, LANES), jnp.float32)
    inc = pl.pallas_call(
        gain_kernel,
        out_shape=jax.ShapeDtypeStruct((NV * NV, NV), jnp.float32),
        in_specs=[pl.BlockSpec(memory_space=pltpu.SMEM)]
        + [pl.BlockSpec(memory_space=pltpu.VMEM)] * 9,
        out_specs=pl.BlockSpec(memory_space=pltpu.VMEM),
        scratch_shapes=[big] * 11 + [pltpu.VMEM((3, NV, LANES), jnp.float32)],
        compiler_params=pltpu.CompilerParams(vmem_limit_bytes=40 * 1024 * 1024),
        cost_estimate=pl.CostEstimate(
            flops=2 * 10**9, bytes_accessed=4 * 10**6, transcendentals=2 * 10**6
        ),
    )(
        rates, doubled, table(f_z), table(f_yx), table(i_z), table(back), table(freq),
        table(lane), table(vel), dirs,
    )
    return inc.reshape(NV, NV * NV)


def flux_kernel(
    slot_ref, kind_ref, coef_ref, normal_ref, vel_ref, x_ref, dist_ref, before_ref, after_ref,
    inflow_ref, out_ref,
):
    faces, cells = kind_ref.shape
    vel_y, vel_z, vel_x = vel_ref[0:1, :], vel_ref[1:2, :], x_ref[...]

    def one_cell(c, carry):
        own = dist_ref[c]
        total = jnp.zeros_like(own)
        for k in range(faces):
            slot = slot_ref[k, c]
            kind = kind_ref[k, c]
            low = before_ref[jnp.clip(slot, 0, cells - 1)]
            mid = dist_ref[jnp.clip(slot - cells, 0, cells - 1)]
            high = after_ref[jnp.clip(slot - 2 * cells, 0, cells - 1)]
            nearby = jnp.where(slot < cells, low, jnp.where(slot < 2 * cells, mid, high))
            upwind = jnp.where(kind == 0, nearby, jnp.where(kind == 1, inflow_ref[...], own))
            dot = normal_ref[0, k, c] * vel_x + (
                normal_ref[1, k, c] * vel_y + normal_ref[2, k, c] * vel_z
            )
            total += coef_ref[k, c] * (
                jnp.maximum(dot, 0.0) * own + jnp.minimum(dot, 0.0) * upwind
            )
        out_ref[c] = own - total
        return carry

    lax.fori_loop(0, cells, one_cell, 0)


def transported(dist, before, after, inflow, slot, kind, coef, angles, slab_x):
    cells, rows, columns = dist.shape
    azimuth, elevation = angles[0], angles[1]
    normal = jnp.stack(
        [
            jnp.cos(azimuth) * jnp.cos(elevation),
            jnp.sin(azimuth) * jnp.cos(elevation),
            jnp.sin(elevation),
        ]
    )
    speed = (2.0 * np.arange(NV) + 1.0 - NV) / NV
    vel = np.stack([np.repeat(speed, NV), np.tile(speed, NV)])
    return pl.pallas_call(
        flux_kernel,
        out_shape=jax.ShapeDtypeStruct(dist.shape, jnp.float32),
        in_specs=[pl.BlockSpec(memory_space=pltpu.SMEM)] * 4
        + [pl.BlockSpec(memory_space=pltpu.VMEM)] * 6,
        out_specs=pl.BlockSpec(memory_space=pltpu.VMEM),
        compiler_params=pltpu.CompilerParams(vmem_limit_bytes=24 * 1024 * 1024),
        cost_estimate=pl.CostEstimate(flops=2 * 10**7, bytes_accessed=3 * 10**6, transcendentals=0),
    )(
        slot, kind, coef, normal, jnp.asarray(vel, jnp.float32), slab_x[:, None],
        dist, before, after, inflow,
    )


def body(
    dist,
    inflow,
    neighbor,
    face_kind,
    member,
    face_coef,
    face_angles,
    dir_angles,
    dir_weights,
    relax_step,
    pen_rate,
):
    cells_dev, slab_rows, columns = dist.shape
    groups = lax.axis_size("vel")
    vel_index = lax.axis_index("vel")
    slab_x = lax.dynamic_slice_in_dim(velocity_grid(NV), vel_index * slab_rows, slab_rows)
    per_device = cells_dev // groups
    blocks = dist.reshape(groups, per_device, slab_rows, columns)
    whole_cells = lax.all_to_all(blocks, "vel", split_axis=0, concat_axis=2, tiled=True).reshape(
        per_device, NV, columns
    )
    before, after = neighbours(dist, "space")
    local_slot = neighbor - (lax.axis_index("space") * cells_dev - cells_dev)
    moved = transported(
        dist, before, after, inflow, local_slot, face_kind, face_coef, face_angles, slab_x
    )
    rates = lax.dynamic_slice_in_dim(
        jnp.stack([relax_step, pen_rate], axis=1), vel_index * per_device, per_device
    )
    increments = jnp.stack(
        [
            collision_step(whole_cells[i].reshape(NV, NV, NV), rates[i], dir_angles, dir_weights)
            for i in range(per_device)
        ]
    )
    increment = lax.all_to_all(
        increments.reshape(1, per_device, NV, columns),
        "vel",
        split_axis=2,
        concat_axis=0,
        tiled=True,
    )
    increment = increment.reshape(cells_dev, slab_rows, columns)
    return jnp.where(member[:, None, None] == 1, moved + increment, dist)


def solution(mesh):
    placed = (
        P("space", "vel", None),
        P("vel", None),
        P(None, "space"),
        P(None, "space"),
        P("space"),
        P(None, "space"),
        P(None, None, "space"),
        P(),
        P(),
        P("space"),
        P("space"),
    )
    return jax.shard_map(
        body, mesh=mesh, in_specs=placed, out_specs=P("space", "vel", None), check_vma=False
    )
```

time: 87.7 us -> 76.9 us (0.88)
  other arithmetic: 9.8 us -> 2.78 us
  between operations: 6.07 us -> 0.36 us
  matrix products: 5.15 us -> 0 us
  waiting for transfers between devices: 5.79 us -> 10 us
  Pallas kernels: 35.4 us -> 39.5 us
    dot_general x1 -> x0, matrix products: 5.15 us -> none  [body(): jnp.dot(onehot.reshape(face_count * cells_dev, 3 * cells_dev), padded.res...]
    pallas_call x1 -> x2, Pallas kernels: 35.4 us -> 39.5 us  [the longest x1 37 us: collision_step(): pl.pallas_call(gain_kernel, out_shape=jax.ShapeDtypeStruct((NV * NV, NV),...]
    reduce_sum x1 -> x0, other arithmetic: 3.59 us -> none  [moment_sums(): jnp.sum(values * vel_z, axis=(-2, -1))]
    all_to_all x1, waiting for transfers between devices: 0.01 us -> 2.93 us  [body(): lax.all_to_all(increments.reshape(1, per_device, NV, columns), 'vel', spl...]
    ppermute x0 -> x2, local copies, waits for them, and re-layouts: none -> 2.22 us  [neighbours(): return (lax.ppermute(shard, axis, up), lax.ppermute(shard, axis, down))]
    another operation x3 -> x4, local copies, waits for them, and re-layouts: 0.83 us -> 2.77 us  [the longest x1 1.94 us: body(): increments.reshape(1, per_device, NV, columns)]
    mul x7 -> x1, other arithmetic: 1.84 us -> 0.05 us  [transported(): jnp.cos(azimuth) * jnp.cos(elevation)]
    dot_general x1 -> x0, local copies, waits for them, and re-layouts: 1.73 us -> none  [body(): jnp.dot(onehot.reshape(face_count * cells_dev, 3 * cells_dev), padded.res...]
  transfers between devices with their start and end apart: 4 -> 4, of which waited for: 1 -> 2; matrix products, arithmetic and copies ran while one was open for 26% -> 12% of each run, Pallas kernels for 41% -> 52%
where the time goes in v1:
time: 76.9 us; the launch traced here: 76.5 us
  Pallas kernels  39.5 us (51%)
  starting transfers between devices  14.3 us (19%)
  waiting for transfers between devices  10 us (13%)
  local copies, waits for them, and re-layouts  9.59 us (12%)
  other arithmetic  2.78 us (4%)
    pallas_call x1, Pallas kernels, collision_step(): pl.pallas_call(gain_kernel, out_shape=jax.ShapeDtypeStruct((NV * NV, NV),...  37 us
    all_to_all x1, waiting for transfers between devices, body(): lax.all_to_all(blocks, 'vel', split_axis=0, concat_axis=2, tiled=True)  7.06 us
    ppermute x2, starting transfers between devices, neighbours(): return (lax.ppermute(shard, axis, up), lax.ppermute(shard, axis, down))  7.02 us
    all_to_all x1, starting transfers between devices, body(): lax.all_to_all(increments.reshape(1, per_device, NV, columns), 'vel', spl...  3.64 us
    all_to_all x1, starting transfers between devices, body(): lax.all_to_all(blocks, 'vel', split_axis=0, concat_axis=2, tiled=True)  3.61 us
    all_to_all x1, waiting for transfers between devices, body(): lax.all_to_all(increments.reshape(1, per_device, NV, columns), 'vel', spl...  2.93 us
    pallas_call x1, Pallas kernels, transported(): pl.pallas_call(flux_kernel, out_shape=jax.ShapeDtypeStruct(dist.shape, jn...  2.44 us
    reshape x1, local copies, waits for them, and re-layouts, body(): blocks = dist.reshape(groups, per_device, slab_rows, columns)  2.23 us
  transfers between devices with their start and end apart: 4, of which 2 were waited for; matrix products, arithmetic and copies ran while one was open for 12% of the time, Pallas kernels for 52%

profile of v1, /device:TPU:0, one launch (start us, length us, event | category | flops | bytes accessed | tf_op | source)
XLA Modules:
  0.0 76.5 jit_solution(11565613458465588826)
XLA Ops:
  0.0 5.7 %collective-permute-start = (f32[4,12,2304]{2,0,1:T(4,128)}, f32[4,12,2304]{2,0,1:T(4,128)}, u32[]{:S(2)}, u32[]{:S(2)}) collective-permute-start(f32[4,12,2304]{2,0,1:T(4,128)} %param.19), channel_id=1, source_target_pairs={{0,4},{4,8},{8,12},{12,16},{16,20},{20,24},{24,28},{1,5},{5,9},{9,... | collective-permute-start | bytes 1327112 | tf_op jit(solution)/shard_map/ppermute | solution.py:20
  5.7 1.3 %collective-permute-start.1 = (f32[4,12,2304]{2,0,1:T(4,128)}, f32[4,12,2304]{2,0,1:T(4,128)}, u32[]{:S(2)}, u32[]{:S(2)}) collective-permute-start(f32[4,12,2304]{2,0,1:T(4,128)} %param.19), channel_id=1, source_target_pairs={{4,0},{8,4},{12,8},{16,12},{20,16},{24,20},{28,24},{5,1},{9,5},{13... | collective-permute-start | bytes 1327112 | tf_op jit(solution)/shard_map/ppermute | solution.py:20
  7.0 2.2 %copy.57 = f32[4,1,12,2304]{3,1,2,0:T(1,128)} copy(f32[4,1,12,2304]{3,0,2,1:T(4,128)} %bitcast.9) | data formatting | bytes 884736 | tf_op jit(solution)/shard_map/reshape | solution.py:307
  9.3 0.0 copy-start.17
  9.3 0.0 copy-start.12
  9.3 3.6 %all-to-all-start = ((f32[4,1,12,2304]{3,1,2,0:T(1,128)}), f32[4,1,12,2304]{3,1,2,0:T(1,128)S(1)}, u32[]{:S(2)}, u32[]{:S(2)}) async-start(f32[4,1,12,2304]{3,1,2,0:T(1,128)} %copy.57), calls=%async_computation | async-start | bytes 884736 | tf_op jit(solution)/shard_map/all_to_all | solution.py:308
  12.9 0.0 copy-done.11
  12.9 0.1 copy.54.dist_ref
  13.0 0.1 dynamic-slice_bitcast_fusion
  13.1 0.1 copy.53.x_ref
  13.2 0.0 copy-done.15
  13.2 0.1 broadcast_in_dim.25
  13.3 0.1 reshape_reshape.3
  13.4 0.0 copy-done.16
  13.4 0.0 copy-done.17
  13.4 0.2 dynamic-slice_reduce_fusion.rates_ref
  13.7 0.1 pad.9.clone
  13.8 7.1 %all-to-all-done = f32[4,1,12,2304]{3,1,2,0:T(1,128)S(1)} async-done(((f32[4,1,12,2304]{3,1,2,0:T(1,128)}), f32[4,1,12,2304]{3,1,2,0:T(1,128)S(1)}, u32[]{:S(2)}, u32[]{:S(2)}) %all-to-all-start) | async-done | bytes 442400 | tf_op jit(solution)/shard_map/all_to_all | solution.py:308
  20.8 1.1 %reduce.1 = f32[4,12,2304]{2,1,0:T(8,128)S(1)} reduce(f32[4,1,12,2304]{3,1,2,0:T(1,128)S(1)} %all-to-all-done, f32[]{:T(128)} %constant.67), dimensions={1}, to_apply=%all_to_all.4.reduce_sub_computation | reduce | bytes 884740 | tf_op jit(solution)/shard_map/all_to_all | solution.py:308
  21.9 0.7 reshape_reshape_squeeze_reshape.3
  22.7 0.0 copy-start.4
  22.7 0.0 copy-start.5
  22.7 0.0 copy-start.6
  22.7 0.0 copy-start.7
  22.7 0.0 copy-start.8
  22.8 0.0 copy-start.9
  22.8 0.0 copy-start.10
  22.8 0.4 maximum_maximum_fusion.cube_ref
  23.2 0.5 copy-done.4
  23.6 0.0 copy-done.5
  23.7 0.0 copy-done.6
  23.7 37.0 %shard_map.182 = f32[2304,48]{1,0:T(8,128)S(1)} custom-call(f32[2]{0:T(128)S(1)} %dynamic-slice_reduce_fusion.rates_ref, f32[2304,128]{1,0:T(8,128)S(1)} %maximum_maximum_fusion.cube_ref, f32[128,256]{1,0:T(8,128)S(1)} %copy-done.5, f32[96,48]{1,0:T(8,128)S(1)} %copy-done.7, f32[256,256]{1,0:T(8,128)S(1)} %copy-done.4, f32[48,48]{1,0:T(8,128)S(1)} %copy-done.8, ...), custom_call_target="tpu_custom_call" | custom-call | flops 2000000000 | bytes 4000000 | tf_op jit(solution)/shard_map/pallas_call | solution.py:215
  60.8 0.0 copy-start.13
  60.8 1.9 %reshape_stack_reshape.4 = f32[1,1,48,2304]{3,1,0,2:T(1,128)} reshape(f32[2304,48]{1,0:T(8,128)S(1)} %shard_map.182) | data formatting | bytes 884736 | tf_op jit(solution)/shard_map/reshape;stack;reshape | solution.py:326
  62.7 3.6 %all-to-all-start.1 = ((f32[1,1,48,2304]{3,1,0,2:T(1,128)}), f32[1,1,48,2304]{3,1,0,2:T(1,128)S(1)}, u32[]{:S(2)}, u32[]{:S(2)}) async-start(f32[1,1,48,2304]{3,1,0,2:T(1,128)} %reshape_stack_reshape.4), calls=%async_computation.1 | async-start | bytes 884736 | tf_op jit(solution)/shard_map/all_to_all | solution.py:325
  66.4 0.0 copy-start
  66.4 0.0 copy-start.1
  66.4 0.0 copy-start.2
  66.4 0.0 copy-start.3
  66.5 0.0 collective-permute-done
  66.5 1.1 %copy.55.before_ref = f32[4,12,2304]{2,1,0:T(8,128)S(1)} copy(f32[4,12,2304]{2,0,1:T(4,128)} %collective-permute-done) | data formatting | bytes 884736 | tf_op jit(solution)/shard_map/ppermute | solution.py:20
  67.6 0.0 collective-permute-done.1
  67.6 1.1 %copy.56.after_ref = f32[4,12,2304]{2,1,0:T(8,128)S(1)} copy(f32[4,12,2304]{2,0,1:T(4,128)} %collective-permute-done.1) | data formatting | bytes 884736 | tf_op jit(solution)/shard_map/ppermute | solution.py:20
  68.8 2.4 %shard_map.181 = f32[4,12,2304]{2,1,0:T(8,128)S(1)} custom-call(s32[4,4]{1,0:T(4,128)S(1)} %broadcast_subtract_fusion.slot_ref, s32[4,4]{1,0:T(4,128)S(1)} %copy-done.2, f32[4,4]{1,0:T(4,128)S(1)} %copy-done.3, f32[3,4,4]{2,1,0:T(4,128)S(1)} %pad_maximum_fusion.normal_ref, f32[2,2304]{1,0:T(2,128)S(1)} %copy-done.1, f32[12,1]{1,0:T(8,128)S(1)} %copy.53.x_ref, ...), custom_call_target="tpu_custom_call" | custom-call | flops 20000000 | bytes 3000000 | tf_op jit(solution)/shard_map/pallas_call | solution.py:275
  71.2 2.9 %all-to-all-done.1 = f32[1,1,48,2304]{3,1,0,2:T(1,128)S(1)} async-done(((f32[1,1,48,2304]{3,1,0,2:T(1,128)}), f32[1,1,48,2304]{3,1,0,2:T(1,128)S(1)}, u32[]{:S(2)}, u32[]{:S(2)}) %all-to-all-start.1) | async-done | bytes 442400 | tf_op jit(solution)/shard_map/all_to_all | solution.py:325
  74.1 1.0 %reduce.2 = f32[48,2304]{1,0:T(8,128)S(1)} reduce(f32[1,1,48,2304]{3,1,0,2:T(1,128)S(1)} %all-to-all-done.1, f32[]{:T(128)} %constant.67), dimensions={0,1}, to_apply=%all_to_all.5.reduce_sub_computation | reduce | bytes 884740 | tf_op jit(solution)/shard_map/all_to_all | solution.py:325
  75.2 0.2 add_select_fusion
  75.4 1.0 %copy.61 = f32[4,12,2304]{2,0,1:T(4,128)} copy(f32[4,12,2304]{2,1,0:T(8,128)S(1)} %add_select_fusion) | data formatting | bytes 884736 | tf_op jit(solution)/shard_map/jit(_where)/select_n | solution.py:333
  (28 shorter events, 0.2 us)
Async XLA Ops:
  0.0 12.9 %copy-start.11 = (f32[4,12,2304]{2,0,1:T(4,128)S(1)}, f32[4,12,2304]{2,0,1:T(4,128)}, u32[]{:S(2)}) copy-start(f32[4,12,2304]{2,0,1:T(4,128)} %param.19) | copy-start | bytes 1327108
  0.0 66.5 %collective-permute-start = (f32[4,12,2304]{2,0,1:T(4,128)}, f32[4,12,2304]{2,0,1:T(4,128)}, u32[]{:S(2)}, u32[]{:S(2)}) collective-permute-start(f32[4,12,2304]{2,0,1:T(4,128)} %param.19), channel_id=1, source_target_pairs={{0,4},{4,8},{8,12},{12,16},{16,20},{20,24},{24,28},{1,5},{5,9},{9,... | collective-permute-start | bytes 1327112 | tf_op jit(solution)/shard_map/ppermute | solution.py:20
  5.7 61.9 %collective-permute-start.1 = (f32[4,12,2304]{2,0,1:T(4,128)}, f32[4,12,2304]{2,0,1:T(4,128)}, u32[]{:S(2)}, u32[]{:S(2)}) collective-permute-start(f32[4,12,2304]{2,0,1:T(4,128)} %param.19), channel_id=1, source_target_pairs={{4,0},{8,4},{12,8},{16,12},{20,16},{24,20},{28,24},{5,1},{9,5},{13... | collective-permute-start | bytes 1327112 | tf_op jit(solution)/shard_map/ppermute | solution.py:20
  9.3 4.0 %copy-start.14 = (f32[2,6]{1,0:T(2,128)S(1)}, f32[2,6]{1,0:T(2,128)}, u32[]{:S(2)}) copy-start(f32[2,6]{1,0:T(2,128)} %param.26) | copy-start | bytes 148
  9.3 4.0 %copy-start.15 = (f32[6]{0:T(128)S(1)}, f32[6]{0:T(128)}, u32[]{:S(2)}) copy-start(f32[6]{0:T(128)} %param.27) | copy-start | bytes 76
  9.3 4.1 %copy-start.18 = (s32[4]{0:T(128)S(1)}, s32[4]{0:T(128)}, u32[]{:S(2)}) copy-start(s32[4]{0:T(128)} %param.23) | copy-start | bytes 52
  9.3 4.1 %copy-start.16 = (f32[4]{0:T(128)S(1)}, f32[4]{0:T(128)}, u32[]{:S(2)}) copy-start(f32[4]{0:T(128)} %param.29) | copy-start | bytes 52
  9.3 4.1 %copy-start.17 = (f32[4]{0:T(128)S(1)}, f32[4]{0:T(128)}, u32[]{:S(2)}) copy-start(f32[4]{0:T(128)} %param.28) | copy-start | bytes 52
  9.3 4.4 %copy-start.12 = (f32[2,4,4]{2,1,0:T(4,128)S(1)}, f32[2,4,4]{2,1,0:T(4,128)}, u32[]{:S(2)}) copy-start(f32[2,4,4]{2,1,0:T(4,128)} %param.25) | copy-start | bytes 388
  9.3 11.5 %all-to-all-start = ((f32[4,1,12,2304]{3,1,2,0:T(1,128)}), f32[4,1,12,2304]{3,1,2,0:T(1,128)S(1)}, u32[]{:S(2)}, u32[]{:S(2)}) async-start(f32[4,1,12,2304]{3,1,2,0:T(1,128)} %copy.57), calls=%async_computation | async-start | bytes 884736 | tf_op jit(solution)/shard_map/all_to_all | solution.py:308
  22.7 1.0 %copy-start.4 = (f32[256,256]{1,0:T(8,128)S(1)}, f32[256,256]{1,0:T(8,128)}, u32[]{:S(2)}) copy-start(f32[256,256]{1,0:T(8,128)} %constant.52.clone.iz_ref) | copy-start | bytes 786436
  22.7 1.0 %copy-start.5 = (f32[128,256]{1,0:T(8,128)S(1)}, f32[128,256]{1,0:T(8,128)}, u32[]{:S(2)}) copy-start(f32[128,256]{1,0:T(8,128)} %constant.50.clone.fz_ref) | copy-start | bytes 393220
  22.7 1.0 %copy-start.6 = (f32[3,48,128]{2,1,0:T(8,128)S(1)}, f32[3,48,128]{2,1,0:T(8,128)}, u32[]{:S(2)}) copy-start(f32[3,48,128]{2,1,0:T(8,128)} %constant.56.clone.vel_ref) | copy-start | bytes 221188
  22.7 1.0 %copy-start.7 = (f32[96,48]{1,0:T(8,128)S(1)}, f32[96,48]{1,0:T(8,128)}, u32[]{:S(2)}) copy-start(f32[96,48]{1,0:T(8,128)} %constant.51.clone.fyx_ref) | copy-start | bytes 55300
  22.7 1.0 %copy-start.8 = (f32[48,48]{1,0:T(8,128)S(1)}, f32[48,48]{1,0:T(8,128)}, u32[]{:S(2)}) copy-start(f32[48,48]{1,0:T(8,128)} %constant.53.clone.iv_ref) | copy-start | bytes 27652
  22.8 1.0 %copy-start.9 = (f32[48,128]{1,0:T(8,128)S(1)}, f32[48,128]{1,0:T(8,128)}, u32[]{:S(2)}) copy-start(f32[48,128]{1,0:T(8,128)} %constant.54.clone.freq_ref) | copy-start | bytes 73732
  22.8 1.0 %copy-start.10 = (f32[1,128]{1,0:T(1,128)S(1)}, f32[1,128]{1,0:T(1,128)}, u32[]{:S(2)}) copy-start(f32[1,128]{1,0:T(1,128)} %constant.55.clone.lane_ref) | copy-start | bytes 1540
  60.8 5.7 %copy-start.13 = (s32[4,4]{1,0:T(4,128)S(1)}, s32[4,4]{1,0:T(4,128)}, u32[]{:S(2)}) copy-start(s32[4,4]{1,0:T(4,128)} %param.21) | copy-start | bytes 196
  62.7 11.4 %all-to-all-start.1 = ((f32[1,1,48,2304]{3,1,0,2:T(1,128)}), f32[1,1,48,2304]{3,1,0,2:T(1,128)S(1)}, u32[]{:S(2)}, u32[]{:S(2)}) async-start(f32[1,1,48,2304]{3,1,0,2:T(1,128)} %reshape_stack_reshape.4), calls=%async_computation.1 | async-start | bytes 884736 | tf_op jit(solution)/shard_map/all_to_all | solution.py:325
  66.4 2.3 %copy-start = (f32[12,2304]{1,0:T(8,128)S(1)}, f32[12,2304]{1,0:T(8,128)}, u32[]{:S(2)}) copy-start(f32[12,2304]{1,0:T(8,128)} %inflow_ref.1) | copy-start | bytes 331780
  66.4 2.3 %copy-start.1 = (f32[2,2304]{1,0:T(2,128)S(1)}, f32[2,2304]{1,0:T(2,128)}, u32[]{:S(2)}) copy-start(f32[2,2304]{1,0:T(2,128)} %constant.49.clone.vel_ref) | copy-start | bytes 55300
  66.4 2.3 %copy-start.2 = (s32[4,4]{1,0:T(4,128)S(1)}, s32[4,4]{1,0:T(4,128)}, u32[]{:S(2)}) copy-start(s32[4,4]{1,0:T(4,128)} %kind_ref.1) | copy-start | bytes 196
  66.4 2.3 %copy-start.3 = (f32[4,4]{1,0:T(4,128)S(1)}, f32[4,4]{1,0:T(4,128)}, u32[]{:S(2)}) copy-start(f32[4,4]{1,0:T(4,128)} %coef_ref.1) | copy-start | bytes 196

commit v2 on v1

--- a/solution.py
+++ b/solution.py
@@ -48,8 +48,39 @@
     return out
 
 
-def dot3(a, b):
-    return jnp.dot(a, b, precision=lax.Precision.HIGH, preferred_element_type=jnp.float32)
+def halves(values):
+    high = values.astype(jnp.bfloat16)
+    return high, (values - high.astype(jnp.float32)).astype(jnp.bfloat16)
+
+
+def constant_halves(matrix):
+    single = np.asarray(matrix, np.float32)
+    high = single.astype(jnp.bfloat16)
+    return high, (single - high.astype(np.float32)).astype(jnp.bfloat16)
+
+
+def right_parts(matrix):
+    return jnp.asarray(np.stack(constant_halves(matrix)))
+
+
+def left_parts(matrix):
+    high, low = constant_halves(matrix)
+    return jnp.asarray(np.concatenate([high, low, high], axis=1))
+
+
+def product(a, b):
+    return jnp.dot(a, b, preferred_element_type=jnp.float32)
+
+
+def by_right(values, parts_ref):
+    high, low = halves(values)
+    main = parts_ref[0]
+    return product(high, main) + (product(low, main) + product(high, parts_ref[1]))
+
+
+def by_left(parts, values):
+    high, low = halves(values)
+    return product(parts, jnp.concatenate([high, high, low], axis=0))
 
 
 def gain_kernel(
@@ -85,9 +116,9 @@
 
     def forward_yz(i, carry):
         rows = pl.multiple_of(i * (CHUNK * n), CHUNK * n)
-        z = dot3(cube_ref[pl.ds(rows, CHUNK * n), :], fz_ref[...])
+        z = by_right(cube_ref[pl.ds(rows, CHUNK * n), :], fz_ref)
         for u in range(CHUNK):
-            out = dot3(fyx_ref[...], z[u * n : (u + 1) * n, :])
+            out = by_left(fyx_ref[...], z[u * n : (u + 1) * n, :])
             here = pl.ds(rows + u * n, n)
             y00[here, :] = out[:n, :LANES]
             y10[here, :] = out[n:, :LANES]
@@ -101,8 +132,8 @@
         for u in range(CHUNK):
             q = i * CHUNK + u
             pick = pl.ds(q, n, stride=n)
-            even = dot3(fyx_ref[:n, :], jnp.concatenate([y00[pick, :], y11[pick, :]], axis=1))
-            odd = dot3(fyx_ref[n:, :], jnp.concatenate([y10[pick, :], y01[pick, :]], axis=1))
+            even = by_left(fyx_ref[:n, :], jnp.concatenate([y00[pick, :], y11[pick, :]], axis=1))
+            odd = by_left(fyx_ref[n:, :], jnp.concatenate([y10[pick, :], y01[pick, :]], axis=1))
             g000, g011 = even[:, :LANES], even[:, LANES:]
             g110, g101 = odd[:, :LANES], odd[:, LANES:]
             here = pl.ds(pl.multiple_of(q * n, n), n)
@@ -150,9 +181,9 @@
                 for kappa, part in ((up + c, f1), (up - c, f2), (um + c, f3), (um - c, f4)):
                     smoothing += jnp.exp(kappa * kappa * (-8.0 / (NV * NV))) * part
                 packed.append(jnp.concatenate([shifting, weight * smoothing], axis=1))
-            z = dot3(jnp.concatenate(packed, axis=0), iz_ref[...])
+            z = by_right(jnp.concatenate(packed, axis=0), iz_ref)
             for u in range(CHUNK):
-                out = dot3(iv_ref[...], z[u * n : (u + 1) * n, :])
+                out = by_left(iv_ref[...], z[u * n : (u + 1) * n, :])
                 here = pl.ds(pl.multiple_of((i * CHUNK + u) * n, n), n)
                 ta[here, :] = out[:, :LANES]
                 tb[here, :] = out[:, LANES:]
@@ -164,7 +195,7 @@
             for u in range(CHUNK):
                 q = i * CHUNK + u
                 pick = pl.ds(q, n, stride=n)
-                out = dot3(iv_ref[...], jnp.concatenate([ta[pick, :], tb[pick, :]], axis=1))
+                out = by_left(iv_ref[...], jnp.concatenate([ta[pick, :], tb[pick, :]], axis=1))
                 here = pl.ds(pl.multiple_of(q * n, n), n)
                 term = out[:, LANES:] * (out[:, :LANES] - cube_ref[here, :])
                 if pack == 0:
@@ -224,7 +255,8 @@
             flops=2 * 10**9, bytes_accessed=4 * 10**6, transcendentals=2 * 10**6
         ),
     )(
-        rates, doubled, table(f_z), table(f_yx), table(i_z), table(back), table(freq),
+        rates, doubled, right_parts(f_z), left_parts(f_yx), right_parts(i_z), left_parts(back),
+        table(freq),
         table(lane), table(vel), dirs,
     )
     return inc.reshape(NV, NV * NV)
@@ -308,7 +340,8 @@
     whole_cells = lax.all_to_all(blocks, "vel", split_axis=0, concat_axis=2, tiled=True).reshape(
         per_device, NV, columns
     )
-    before, after = neighbours(dist, "space")
+    halo_source, whole_cells = lax.optimization_barrier((dist, whole_cells))
+    before, after = neighbours(halo_source, "space")
     local_slot = neighbor - (lax.axis_index("space") * cells_dev - cells_dev)
     moved = transported(
         dist, before, after, inflow, local_slot, face_kind, face_coef, face_angles, slab_x

time: 76.9 us -> 73.6 us (0.957)
  Pallas kernels: 39.5 us -> 32.4 us
  waiting for transfers between devices: 10 us -> 14.8 us
  local copies, waits for them, and re-layouts: 9.59 us -> 8.68 us
    pallas_call x1, Pallas kernels: 37 us -> 30 us  [collision_step(): pl.pallas_call(gain_kernel, out_shape=jax.ShapeDtypeStruct((NV * NV, NV),...]
    all_to_all x1, waiting for transfers between devices: 2.93 us -> 7.72 us  [body(): lax.all_to_all(increments.reshape(1, per_device, NV, columns), 'vel', spl...]
    all_to_all x1 -> x0, other arithmetic: 1.08 us -> none  [body(): lax.all_to_all(blocks, 'vel', split_axis=0, concat_axis=2, tiled=True)]
    optimization_barrier x0 -> x1, other arithmetic: none -> 1.06 us  [body(): halo_source, whole_cells = lax.optimization_barrier((dist, whole_cells))]
    ppermute x2, local copies, waits for them, and re-layouts: 2.22 us -> 1.25 us  [neighbours(): return (lax.ppermute(shard, axis, up), lax.ppermute(shard, axis, down))]
    ppermute x2, starting transfers between devices: 7.02 us -> 6.09 us  [neighbours(): return (lax.ppermute(shard, axis, up), lax.ppermute(shard, axis, down))]
    all_to_all x1, starting transfers between devices: 3.61 us -> 4.38 us  [body(): lax.all_to_all(blocks, 'vel', split_axis=0, concat_axis=2, tiled=True)]
  transfers between devices with their start and end apart: 4 -> 4, of which waited for: 2 -> 2; matrix products, arithmetic and copies ran while one was open for 12% -> 10% of each run, Pallas kernels for 52% -> 41%
where the time goes in v2:
time: 73.6 us; the launch traced here: 73.2 us
  Pallas kernels  32.4 us (44%)
  waiting for transfers between devices  14.8 us (20%)
  starting transfers between devices  14.1 us (19%)
  local copies, waits for them, and re-layouts  8.68 us (12%)
  other arithmetic  2.8 us (4%)
    pallas_call x1, Pallas kernels, collision_step(): pl.pallas_call(gain_kernel, out_shape=jax.ShapeDtypeStruct((NV * NV, NV),...  30 us
    all_to_all x1, waiting for transfers between devices, body(): lax.all_to_all(increments.reshape(1, per_device, NV, columns), 'vel', spl...  7.72 us
    all_to_all x1, waiting for transfers between devices, body(): lax.all_to_all(blocks, 'vel', split_axis=0, concat_axis=2, tiled=True)  7.11 us
    ppermute x2, starting transfers between devices, neighbours(): return (lax.ppermute(shard, axis, up), lax.ppermute(shard, axis, down))  6.09 us
    all_to_all x1, starting transfers between devices, body(): lax.all_to_all(blocks, 'vel', split_axis=0, concat_axis=2, tiled=True)  4.38 us
    all_to_all x1, starting transfers between devices, body(): lax.all_to_all(increments.reshape(1, per_device, NV, columns), 'vel', spl...  3.64 us
    pallas_call x1, Pallas kernels, transported(): pl.pallas_call(flux_kernel, out_shape=jax.ShapeDtypeStruct(dist.shape, jn...  2.44 us
    reshape x1, local copies, waits for them, and re-layouts, body(): blocks = dist.reshape(groups, per_device, slab_rows, columns)  2.3 us
  transfers between devices with their start and end apart: 4, of which 2 were waited for; matrix products, arithmetic and copies ran while one was open for 10% of the time, Pallas kernels for 41%

profile of v2, /device:TPU:0, one launch (start us, length us, event | category | flops | bytes accessed | tf_op | source)
XLA Modules:
  0.0 73.2 jit_solution(14251777022789544946)
XLA Ops:
  0.0 2.3 %copy.52 = f32[4,1,12,2304]{3,1,2,0:T(1,128)} copy(f32[4,1,12,2304]{3,0,2,1:T(4,128)} %bitcast.10) | data formatting | bytes 884736 | tf_op jit(solution)/shard_map/reshape | solution.py:339
  2.3 0.0 copy-start.17
  2.3 0.0 copy-start.12
  2.3 4.4 %all-to-all-start = ((f32[4,1,12,2304]{3,1,2,0:T(1,128)}), f32[4,1,12,2304]{3,1,2,0:T(1,128)S(1)}, u32[]{:S(2)}, u32[]{:S(2)}) async-start(f32[4,1,12,2304]{3,1,2,0:T(1,128)} %copy.52), calls=%async_computation | async-start | bytes 884736 | tf_op jit(solution)/shard_map/all_to_all | solution.py:340
  6.7 0.0 copy-done.11
  6.7 0.1 copy.54.dist_ref
  6.8 0.1 dynamic-slice_bitcast_fusion
  6.9 0.1 copy.53.x_ref
  7.0 0.0 copy-done.15
  7.0 0.1 broadcast_in_dim.25
  7.1 0.1 reshape_reshape.3
  7.2 0.2 dynamic-slice_reduce_fusion.rates_ref
  7.4 0.1 pad.9.clone
  7.5 0.0 copy-done.12
  7.6 7.1 %all-to-all-done = f32[4,1,12,2304]{3,1,2,0:T(1,128)S(1)} async-done(((f32[4,1,12,2304]{3,1,2,0:T(1,128)}), f32[4,1,12,2304]{3,1,2,0:T(1,128)S(1)}, u32[]{:S(2)}, u32[]{:S(2)}) %all-to-all-start) | async-done | bytes 442400 | tf_op jit(solution)/shard_map/all_to_all | solution.py:340
  14.7 4.8 %collective-permute-start = (f32[4,12,2304]{2,0,1:T(4,128)S(1)}, f32[4,12,2304]{2,0,1:T(4,128)}, u32[]{:S(2)}, u32[]{:S(2)}) collective-permute-start(f32[4,12,2304]{2,0,1:T(4,128)S(1)} %copy-done.11), channel_id=1, source_target_pairs={{0,4},{4,8},{8,12},{12,16},{16,20},{20,24},{24,28},{1,5},{5,9},{9,... | collective-permute-start | bytes 1327112 | tf_op jit(solution)/shard_map/ppermute | solution.py:20
  19.5 1.3 %collective-permute-start.1 = (f32[4,12,2304]{2,0,1:T(4,128)S(1)}, f32[4,12,2304]{2,0,1:T(4,128)S(1)}, u32[]{:S(2)}, u32[]{:S(2)}) collective-permute-start(f32[4,12,2304]{2,0,1:T(4,128)S(1)} %copy-done.11), channel_id=1, source_target_pairs={{4,0},{8,4},{12,8},{16,12},{20,16},{24,20},{28,24},{5,1},{9,5},{13... | collective-permute-start | bytes 1327112 | tf_op jit(solution)/shard_map/ppermute | solution.py:20
  20.8 1.1 %reduce.1 = f32[48,2304]{1,0:T(8,128)S(1)} reduce(f32[1,48,2304]{2,0,1:T(1,128)S(1)} %bitcast.11, f32[]{:T(128)} %constant.67), dimensions={0}, to_apply=%get-tuple-element.8.reduce_sub_computation | reduce | bytes 884740 | tf_op jit(solution)/shard_map/optimization_barrier | solution.py:343
  21.9 0.7 %reshape_reshape_squeeze.3 = f32[2304,48]{1,0:T(8,128)S(1)} reshape(f32[48,2304]{1,0:T(8,128)S(1)} %reduce.1) | data formatting | bytes 884736 | tf_op jit(solution)/shard_map/reshape;reshape;squeeze | solution.py:240
  22.6 0.0 copy-start.4
  22.6 0.0 copy-start.5
  22.6 0.0 copy-start.6
  22.6 0.0 copy-start.7
  22.7 0.0 copy-start.8
  22.7 0.0 copy-start.9
  22.7 0.0 copy-start.10
  22.7 0.4 maximum_maximum_fusion.cube_ref
  23.1 0.5 copy-done.4
  23.6 0.0 copy-done.5
  23.6 0.0 copy-done.6
  23.6 0.0 copy-done.7
  23.6 30.0 %shard_map.182 = f32[2304,48]{1,0:T(8,128)S(1)} custom-call(f32[2]{0:T(128)S(1)} %dynamic-slice_reduce_fusion.rates_ref, f32[2304,128]{1,0:T(8,128)S(1)} %maximum_maximum_fusion.cube_ref, bf16[2,128,256]{2,1,0:T(8,128)(2,1)S(1)} %copy-done.5, bf16[96,144]{1,0:T(8,128)(2,1)S(1)} %copy-done.7, bf16[2,256,256]{2,1,0:T(8,128)(2,1)S(1)} %copy-done.4, ...), custom_call_target="tpu_custom_call" | custom-call | flops 2000000000 | bytes 4000000 | tf_op jit(solution)/shard_map/pallas_call | solution.py:246
  53.7 0.0 copy-start.13
  53.7 1.9 %reshape_stack_reshape.4 = f32[1,1,48,2304]{3,1,0,2:T(1,128)} reshape(f32[2304,48]{1,0:T(8,128)S(1)} %shard_map.182) | data formatting | bytes 884736 | tf_op jit(solution)/shard_map/reshape;stack;reshape | solution.py:359
  55.6 3.6 %all-to-all-start.1 = ((f32[1,1,48,2304]{3,1,0,2:T(1,128)}), f32[1,1,48,2304]{3,1,0,2:T(1,128)S(1)}, u32[]{:S(2)}, u32[]{:S(2)}) async-start(f32[1,1,48,2304]{3,1,0,2:T(1,128)} %reshape_stack_reshape.4), calls=%async_computation.1 | async-start | bytes 884736 | tf_op jit(solution)/shard_map/all_to_all | solution.py:358
  59.3 7.7 %all-to-all-done.1 = f32[1,1,48,2304]{3,1,0,2:T(1,128)S(1)} async-done(((f32[1,1,48,2304]{3,1,0,2:T(1,128)}), f32[1,1,48,2304]{3,1,0,2:T(1,128)S(1)}, u32[]{:S(2)}, u32[]{:S(2)}) %all-to-all-start.1) | async-done | bytes 442400 | tf_op jit(solution)/shard_map/all_to_all | solution.py:358
  67.0 1.1 %reduce.2 = f32[48,2304]{1,0:T(8,128)S(1)} reduce(f32[1,1,48,2304]{3,1,0,2:T(1,128)S(1)} %all-to-all-done.1, f32[]{:T(128)} %constant.67), dimensions={0,1}, to_apply=%all_to_all.5.reduce_sub_computation | reduce | bytes 884740 | tf_op jit(solution)/shard_map/all_to_all | solution.py:358
  68.1 0.0 copy-start
  68.1 0.0 copy-start.1
  68.2 0.0 copy-start.2
  68.2 0.0 copy-start.3
  68.2 0.0 collective-permute-done
  68.2 1.2 %copy.55.before_ref = f32[4,12,2304]{2,1,0:T(8,128)S(1)} copy(f32[4,12,2304]{2,0,1:T(4,128)} %collective-permute-done) | data formatting | bytes 884736 | tf_op jit(solution)/shard_map/ppermute | solution.py:20
  69.3 0.0 collective-permute-done.1
  69.4 0.1 copy.56.after_ref
  69.5 2.4 %shard_map.181 = f32[4,12,2304]{2,1,0:T(8,128)S(1)} custom-call(s32[4,4]{1,0:T(4,128)S(1)} %broadcast_subtract_fusion.slot_ref, s32[4,4]{1,0:T(4,128)S(1)} %copy-done.2, f32[4,4]{1,0:T(4,128)S(1)} %copy-done.3, f32[3,4,4]{2,1,0:T(4,128)S(1)} %pad_maximum_fusion.normal_ref, f32[2,2304]{1,0:T(2,128)S(1)} %copy-done.1, f32[12,1]{1,0:T(8,128)S(1)} %copy.53.x_ref, ...), custom_call_target="tpu_custom_call" | custom-call | flops 20000000 | bytes 3000000 | tf_op jit(solution)/shard_map/pallas_call | solution.py:307
  71.9 0.2 add_select_fusion
  72.2 1.0 %copy.60 = f32[4,12,2304]{2,0,1:T(4,128)} copy(f32[4,12,2304]{2,1,0:T(8,128)S(1)} %add_select_fusion) | data formatting | bytes 884736 | tf_op jit(solution)/shard_map/jit(_where)/select_n | solution.py:366
  (28 shorter events, 0.2 us)
Async XLA Ops:
  0.0 6.7 %copy-start.11 = (f32[4,12,2304]{2,0,1:T(4,128)S(1)}, f32[4,12,2304]{2,0,1:T(4,128)}, u32[]{:S(2)}) copy-start(f32[4,12,2304]{2,0,1:T(4,128)} %param.19) | copy-start | bytes 1327108
  2.3 4.7 %copy-start.14 = (f32[2,6]{1,0:T(2,128)S(1)}, f32[2,6]{1,0:T(2,128)}, u32[]{:S(2)}) copy-start(f32[2,6]{1,0:T(2,128)} %param.26) | copy-start | bytes 148
  2.3 4.7 %copy-start.15 = (f32[6]{0:T(128)S(1)}, f32[6]{0:T(128)}, u32[]{:S(2)}) copy-start(f32[6]{0:T(128)} %param.27) | copy-start | bytes 76
  2.3 4.9 %copy-start.18 = (s32[4]{0:T(128)S(1)}, s32[4]{0:T(128)}, u32[]{:S(2)}) copy-start(s32[4]{0:T(128)} %param.23) | copy-start | bytes 52
  2.3 4.9 %copy-start.16 = (f32[4]{0:T(128)S(1)}, f32[4]{0:T(128)}, u32[]{:S(2)}) copy-start(f32[4]{0:T(128)} %param.29) | copy-start | bytes 52
  2.3 4.9 %copy-start.17 = (f32[4]{0:T(128)S(1)}, f32[4]{0:T(128)}, u32[]{:S(2)}) copy-start(f32[4]{0:T(128)} %param.28) | copy-start | bytes 52
  2.3 5.2 %copy-start.12 = (f32[2,4,4]{2,1,0:T(4,128)S(1)}, f32[2,4,4]{2,1,0:T(4,128)}, u32[]{:S(2)}) copy-start(f32[2,4,4]{2,1,0:T(4,128)} %param.25) | copy-start | bytes 388
  2.3 12.3 %all-to-all-start = ((f32[4,1,12,2304]{3,1,2,0:T(1,128)}), f32[4,1,12,2304]{3,1,2,0:T(1,128)S(1)}, u32[]{:S(2)}, u32[]{:S(2)}) async-start(f32[4,1,12,2304]{3,1,2,0:T(1,128)} %copy.52), calls=%async_computation | async-start | bytes 884736 | tf_op jit(solution)/shard_map/all_to_all | solution.py:340
  14.7 53.5 %collective-permute-start = (f32[4,12,2304]{2,0,1:T(4,128)S(1)}, f32[4,12,2304]{2,0,1:T(4,128)}, u32[]{:S(2)}, u32[]{:S(2)}) collective-permute-start(f32[4,12,2304]{2,0,1:T(4,128)S(1)} %copy-done.11), channel_id=1, source_target_pairs={{0,4},{4,8},{8,12},{12,16},{16,20},{20,24},{24,28},{1,5},{5,9},{9,... | collective-permute-start | bytes 1327112 | tf_op jit(solution)/shard_map/ppermute | solution.py:20
  19.5 49.9 %collective-permute-start.1 = (f32[4,12,2304]{2,0,1:T(4,128)S(1)}, f32[4,12,2304]{2,0,1:T(4,128)S(1)}, u32[]{:S(2)}, u32[]{:S(2)}) collective-permute-start(f32[4,12,2304]{2,0,1:T(4,128)S(1)} %copy-done.11), channel_id=1, source_target_pairs={{4,0},{8,4},{12,8},{16,12},{20,16},{24,20},{28,24},{5,1},{9,5},{13... | collective-permute-start | bytes 1327112 | tf_op jit(solution)/shard_map/ppermute | solution.py:20
  22.6 1.0 %copy-start.4 = (bf16[2,256,256]{2,1,0:T(8,128)(2,1)S(1)}, bf16[2,256,256]{2,1,0:T(8,128)(2,1)}, u32[]{:S(2)}) copy-start(bf16[2,256,256]{2,1,0:T(8,128)(2,1)} %constant.52.clone.iz_ref) | copy-start | bytes 786436
  22.6 1.0 %copy-start.5 = (bf16[2,128,256]{2,1,0:T(8,128)(2,1)S(1)}, bf16[2,128,256]{2,1,0:T(8,128)(2,1)}, u32[]{:S(2)}) copy-start(bf16[2,128,256]{2,1,0:T(8,128)(2,1)} %constant.50.clone.fz_ref) | copy-start | bytes 393220
  22.6 1.0 %copy-start.6 = (f32[3,48,128]{2,1,0:T(8,128)S(1)}, f32[3,48,128]{2,1,0:T(8,128)}, u32[]{:S(2)}) copy-start(f32[3,48,128]{2,1,0:T(8,128)} %constant.56.clone.vel_ref) | copy-start | bytes 221188
  22.6 1.0 %copy-start.7 = (bf16[96,144]{1,0:T(8,128)(2,1)S(1)}, bf16[96,144]{1,0:T(8,128)(2,1)}, u32[]{:S(2)}) copy-start(bf16[96,144]{1,0:T(8,128)(2,1)} %constant.51.clone.fyx_ref) | copy-start | bytes 82948
  22.7 1.0 %copy-start.8 = (bf16[48,144]{1,0:T(8,128)(2,1)S(1)}, bf16[48,144]{1,0:T(8,128)(2,1)}, u32[]{:S(2)}) copy-start(bf16[48,144]{1,0:T(8,128)(2,1)} %constant.53.clone.iv_ref) | copy-start | bytes 41476
  22.7 1.0 %copy-start.9 = (f32[48,128]{1,0:T(8,128)S(1)}, f32[48,128]{1,0:T(8,128)}, u32[]{:S(2)}) copy-start(f32[48,128]{1,0:T(8,128)} %constant.54.clone.freq_ref) | copy-start | bytes 73732
  22.7 1.0 %copy-start.10 = (f32[1,128]{1,0:T(1,128)S(1)}, f32[1,128]{1,0:T(1,128)}, u32[]{:S(2)}) copy-start(f32[1,128]{1,0:T(1,128)} %constant.55.clone.lane_ref) | copy-start | bytes 1540
  53.7 5.6 %copy-start.13 = (s32[4,4]{1,0:T(4,128)S(1)}, s32[4,4]{1,0:T(4,128)}, u32[]{:S(2)}) copy-start(s32[4,4]{1,0:T(4,128)} %param.21) | copy-start | bytes 196
  55.6 11.4 %all-to-all-start.1 = ((f32[1,1,48,2304]{3,1,0,2:T(1,128)}), f32[1,1,48,2304]{3,1,0,2:T(1,128)S(1)}, u32[]{:S(2)}, u32[]{:S(2)}) async-start(f32[1,1,48,2304]{3,1,0,2:T(1,128)} %reshape_stack_reshape.4), calls=%async_computation.1 | async-start | bytes 884736 | tf_op jit(solution)/shard_map/all_to_all | solution.py:358
  68.1 1.3 %copy-start = (f32[12,2304]{1,0:T(8,128)S(1)}, f32[12,2304]{1,0:T(8,128)}, u32[]{:S(2)}) copy-start(f32[12,2304]{1,0:T(8,128)} %inflow_ref.1) | copy-start | bytes 331780
  68.1 1.3 %copy-start.1 = (f32[2,2304]{1,0:T(2,128)S(1)}, f32[2,2304]{1,0:T(2,128)}, u32[]{:S(2)}) copy-start(f32[2,2304]{1,0:T(2,128)} %constant.49.clone.vel_ref) | copy-start | bytes 55300
  68.2 1.3 %copy-start.2 = (s32[4,4]{1,0:T(4,128)S(1)}, s32[4,4]{1,0:T(4,128)}, u32[]{:S(2)}) copy-start(s32[4,4]{1,0:T(4,128)} %kind_ref.1) | copy-start | bytes 196
  68.2 1.3 %copy-start.3 = (f32[4,4]{1,0:T(4,128)S(1)}, f32[4,4]{1,0:T(4,128)}, u32[]{:S(2)}) copy-start(f32[4,4]{1,0:T(4,128)} %coef_ref.1) | copy-start | bytes 196

commit v3 on v2

--- a/solution.py
+++ b/solution.py
@@ -10,7 +10,7 @@
 
 NV = 48
 LANES = 128
-CHUNK = 8
+CHUNK = 24
 
 
 def neighbours(shard, axis):
@@ -340,8 +340,7 @@
     whole_cells = lax.all_to_all(blocks, "vel", split_axis=0, concat_axis=2, tiled=True).reshape(
         per_device, NV, columns
     )
-    halo_source, whole_cells = lax.optimization_barrier((dist, whole_cells))
-    before, after = neighbours(halo_source, "space")
+    before, after = neighbours(dist, "space")
     local_slot = neighbor - (lax.axis_index("space") * cells_dev - cells_dev)
     moved = transported(
         dist, before, after, inflow, local_slot, face_kind, face_coef, face_angles, slab_x

time: 73.6 us -> 62.5 us (0.85)
  Pallas kernels: 32.4 us -> 25.1 us
  waiting for transfers between devices: 14.8 us -> 10.2 us
  local copies, waits for them, and re-layouts: 8.68 us -> 9.59 us
    pallas_call x1, Pallas kernels: 30 us -> 22.6 us  [collision_step(): pl.pallas_call(gain_kernel, out_shape=jax.ShapeDtypeStruct((NV * NV, NV),...]
    all_to_all x1, waiting for transfers between devices: 7.72 us -> 3.11 us  [body(): lax.all_to_all(increments.reshape(1, per_device, NV, columns), 'vel', spl...]
    all_to_all x0 -> x1, other arithmetic: none -> 1.08 us  [body(): lax.all_to_all(blocks, 'vel', split_axis=0, concat_axis=2, tiled=True)]
    optimization_barrier x1 -> x0, other arithmetic: 1.06 us -> none  [body(): halo_source, whole_cells = lax.optimization_barrier((dist, whole_cells))]
    ppermute x2, local copies, waits for them, and re-layouts: 1.25 us -> 2.22 us  [neighbours(): return (lax.ppermute(shard, axis, up), lax.ppermute(shard, axis, down))]
    ppermute x2, starting transfers between devices: 6.09 us -> 7.02 us  [neighbours(): return (lax.ppermute(shard, axis, up), lax.ppermute(shard, axis, down))]
    all_to_all x1, starting transfers between devices: 4.38 us -> 3.61 us  [body(): lax.all_to_all(blocks, 'vel', split_axis=0, concat_axis=2, tiled=True)]
  transfers between devices with their start and end apart: 4 -> 4, of which waited for: 2 -> 2; matrix products, arithmetic and copies ran while one was open for 10% -> 15% of each run, Pallas kernels for 41% -> 40%
where the time goes in v3:
time: 62.5 us; the launch traced here: 62.1 us
  Pallas kernels  25.1 us (40%)
  starting transfers between devices  14.1 us (23%)
  waiting for transfers between devices  10.2 us (16%)
  local copies, waits for them, and re-layouts  9.59 us (15%)
  other arithmetic  2.78 us (4%)
    pallas_call x1, Pallas kernels, collision_step(): pl.pallas_call(gain_kernel, out_shape=jax.ShapeDtypeStruct((NV * NV, NV),...  22.6 us
    all_to_all x1, waiting for transfers between devices, body(): lax.all_to_all(blocks, 'vel', split_axis=0, concat_axis=2, tiled=True)  7.06 us
    ppermute x2, starting transfers between devices, neighbours(): return (lax.ppermute(shard, axis, up), lax.ppermute(shard, axis, down))  7.02 us
    all_to_all x1, starting transfers between devices, body(): lax.all_to_all(blocks, 'vel', split_axis=0, concat_axis=2, tiled=True)  3.61 us
    all_to_all x1, starting transfers between devices, body(): lax.all_to_all(increments.reshape(1, per_device, NV, columns), 'vel', spl...  3.46 us
    all_to_all x1, waiting for transfers between devices, body(): lax.all_to_all(increments.reshape(1, per_device, NV, columns), 'vel', spl...  3.11 us
    pallas_call x1, Pallas kernels, transported(): pl.pallas_call(flux_kernel, out_shape=jax.ShapeDtypeStruct(dist.shape, jn...  2.44 us
    reshape x1, local copies, waits for them, and re-layouts, body(): blocks = dist.reshape(groups, per_device, slab_rows, columns)  2.23 us
  transfers between devices with their start and end apart: 4, of which 2 were waited for; matrix products, arithmetic and copies ran while one was open for 15% of the time, Pallas kernels for 40%

profile of v3, /device:TPU:0, one launch (start us, length us, event | category | flops | bytes accessed | tf_op | source)
XLA Modules:
  0.0 62.1 jit_solution(1374198485799025861)
XLA Ops:
  0.0 5.7 %collective-permute-start = (f32[4,12,2304]{2,0,1:T(4,128)}, f32[4,12,2304]{2,0,1:T(4,128)}, u32[]{:S(2)}, u32[]{:S(2)}) collective-permute-start(f32[4,12,2304]{2,0,1:T(4,128)} %param.19), channel_id=1, source_target_pairs={{0,4},{4,8},{8,12},{12,16},{16,20},{20,24},{24,28},{1,5},{5,9},{9,... | collective-permute-start | bytes 1327112 | tf_op jit(solution)/shard_map/ppermute | solution.py:20
  5.7 1.3 %collective-permute-start.1 = (f32[4,12,2304]{2,0,1:T(4,128)}, f32[4,12,2304]{2,0,1:T(4,128)}, u32[]{:S(2)}, u32[]{:S(2)}) collective-permute-start(f32[4,12,2304]{2,0,1:T(4,128)} %param.19), channel_id=1, source_target_pairs={{4,0},{8,4},{12,8},{16,12},{20,16},{24,20},{28,24},{5,1},{9,5},{13... | collective-permute-start | bytes 1327112 | tf_op jit(solution)/shard_map/ppermute | solution.py:20
  7.0 2.2 %copy.57 = f32[4,1,12,2304]{3,1,2,0:T(1,128)} copy(f32[4,1,12,2304]{3,0,2,1:T(4,128)} %bitcast.9) | data formatting | bytes 884736 | tf_op jit(solution)/shard_map/reshape | solution.py:339
  9.3 0.0 copy-start.17
  9.3 0.0 copy-start.12
  9.3 3.6 %all-to-all-start = ((f32[4,1,12,2304]{3,1,2,0:T(1,128)}), f32[4,1,12,2304]{3,1,2,0:T(1,128)S(1)}, u32[]{:S(2)}, u32[]{:S(2)}) async-start(f32[4,1,12,2304]{3,1,2,0:T(1,128)} %copy.57), calls=%async_computation | async-start | bytes 884736 | tf_op jit(solution)/shard_map/all_to_all | solution.py:340
  12.9 0.0 copy-done.11
  12.9 0.1 copy.54.dist_ref
  13.0 0.1 dynamic-slice_bitcast_fusion
  13.1 0.1 copy.53.x_ref
  13.2 0.0 copy-done.15
  13.2 0.1 broadcast_in_dim.25
  13.3 0.1 reshape_reshape.3
  13.4 0.0 copy-done.16
  13.4 0.0 copy-done.17
  13.4 0.2 dynamic-slice_reduce_fusion.rates_ref
  13.7 0.1 pad.9.clone
  13.8 7.1 %all-to-all-done = f32[4,1,12,2304]{3,1,2,0:T(1,128)S(1)} async-done(((f32[4,1,12,2304]{3,1,2,0:T(1,128)}), f32[4,1,12,2304]{3,1,2,0:T(1,128)S(1)}, u32[]{:S(2)}, u32[]{:S(2)}) %all-to-all-start) | async-done | bytes 442400 | tf_op jit(solution)/shard_map/all_to_all | solution.py:340
  20.8 1.1 %reduce.1 = f32[4,12,2304]{2,1,0:T(8,128)S(1)} reduce(f32[4,1,12,2304]{3,1,2,0:T(1,128)S(1)} %all-to-all-done, f32[]{:T(128)} %constant.67), dimensions={1}, to_apply=%all_to_all.4.reduce_sub_computation | reduce | bytes 884740 | tf_op jit(solution)/shard_map/all_to_all | solution.py:340
  21.9 0.7 %reshape_reshape_squeeze_reshape.3 = f32[2304,48]{1,0:T(8,128)S(1)} reshape(f32[4,12,2304]{2,1,0:T(8,128)S(1)} %reduce.1) | data formatting | bytes 884736 | tf_op jit(solution)/shard_map/reshape;reshape;squeeze;reshape | solution.py:240
  22.7 0.0 copy-start.4
  22.7 0.0 copy-start.5
  22.7 0.0 copy-start.6
  22.7 0.0 copy-start.7
  22.7 0.0 copy-start.8
  22.8 0.0 copy-start.9
  22.8 0.0 copy-start.10
  22.8 0.4 maximum_maximum_fusion.cube_ref
  23.2 0.5 copy-done.4
  23.6 0.0 copy-done.5
  23.7 0.0 copy-done.6
  23.7 22.6 %shard_map.182 = f32[2304,48]{1,0:T(8,128)S(1)} custom-call(f32[2]{0:T(128)S(1)} %dynamic-slice_reduce_fusion.rates_ref, f32[2304,128]{1,0:T(8,128)S(1)} %maximum_maximum_fusion.cube_ref, bf16[2,128,256]{2,1,0:T(8,128)(2,1)S(1)} %copy-done.5, bf16[96,144]{1,0:T(8,128)(2,1)S(1)} %copy-done.7, bf16[2,256,256]{2,1,0:T(8,128)(2,1)S(1)} %copy-done.4, ...), custom_call_target="tpu_custom_call" | custom-call | flops 2000000000 | bytes 4000000 | tf_op jit(solution)/shard_map/pallas_call | solution.py:246
  46.4 0.0 copy-start.13
  46.4 1.9 %reshape_stack_reshape.4 = f32[1,1,48,2304]{3,1,0,2:T(1,128)} reshape(f32[2304,48]{1,0:T(8,128)S(1)} %shard_map.182) | data formatting | bytes 884736 | tf_op jit(solution)/shard_map/reshape;stack;reshape | solution.py:358
  48.3 3.5 %all-to-all-start.1 = ((f32[1,1,48,2304]{3,1,0,2:T(1,128)}), f32[1,1,48,2304]{3,1,0,2:T(1,128)S(1)}, u32[]{:S(2)}, u32[]{:S(2)}) async-start(f32[1,1,48,2304]{3,1,0,2:T(1,128)} %reshape_stack_reshape.4), calls=%async_computation.1 | async-start | bytes 884736 | tf_op jit(solution)/shard_map/all_to_all | solution.py:357
  51.8 0.0 copy-start
  51.8 0.0 copy-start.1
  51.8 0.0 copy-start.2
  51.8 0.0 copy-start.3
  51.9 0.0 collective-permute-done
  51.9 1.1 %copy.55.before_ref = f32[4,12,2304]{2,1,0:T(8,128)S(1)} copy(f32[4,12,2304]{2,0,1:T(4,128)} %collective-permute-done) | data formatting | bytes 884736 | tf_op jit(solution)/shard_map/ppermute | solution.py:20
  53.0 0.0 collective-permute-done.1
  53.0 1.1 %copy.56.after_ref = f32[4,12,2304]{2,1,0:T(8,128)S(1)} copy(f32[4,12,2304]{2,0,1:T(4,128)} %collective-permute-done.1) | data formatting | bytes 884736 | tf_op jit(solution)/shard_map/ppermute | solution.py:20
  54.2 2.4 %shard_map.181 = f32[4,12,2304]{2,1,0:T(8,128)S(1)} custom-call(s32[4,4]{1,0:T(4,128)S(1)} %broadcast_subtract_fusion.slot_ref, s32[4,4]{1,0:T(4,128)S(1)} %copy-done.2, f32[4,4]{1,0:T(4,128)S(1)} %copy-done.3, f32[3,4,4]{2,1,0:T(4,128)S(1)} %pad_maximum_fusion.normal_ref, f32[2,2304]{1,0:T(2,128)S(1)} %copy-done.1, f32[12,1]{1,0:T(8,128)S(1)} %copy.53.x_ref, ...), custom_call_target="tpu_custom_call" | custom-call | flops 20000000 | bytes 3000000 | tf_op jit(solution)/shard_map/pallas_call | solution.py:307
  56.6 3.1 %all-to-all-done.1 = f32[1,1,48,2304]{3,1,0,2:T(1,128)S(1)} async-done(((f32[1,1,48,2304]{3,1,0,2:T(1,128)}), f32[1,1,48,2304]{3,1,0,2:T(1,128)S(1)}, u32[]{:S(2)}, u32[]{:S(2)}) %all-to-all-start.1) | async-done | bytes 442400 | tf_op jit(solution)/shard_map/all_to_all | solution.py:357
  59.7 1.0 %reduce.2 = f32[48,2304]{1,0:T(8,128)S(1)} reduce(f32[1,1,48,2304]{3,1,0,2:T(1,128)S(1)} %all-to-all-done.1, f32[]{:T(128)} %constant.67), dimensions={0,1}, to_apply=%all_to_all.5.reduce_sub_computation | reduce | bytes 884740 | tf_op jit(solution)/shard_map/all_to_all | solution.py:357
  60.8 0.2 add_select_fusion
  61.0 1.0 %copy.61 = f32[4,12,2304]{2,0,1:T(4,128)} copy(f32[4,12,2304]{2,1,0:T(8,128)S(1)} %add_select_fusion) | data formatting | bytes 884736 | tf_op jit(solution)/shard_map/jit(_where)/select_n | solution.py:365
  (28 shorter events, 0.2 us)
Async XLA Ops:
  0.0 12.9 %copy-start.11 = (f32[4,12,2304]{2,0,1:T(4,128)S(1)}, f32[4,12,2304]{2,0,1:T(4,128)}, u32[]{:S(2)}) copy-start(f32[4,12,2304]{2,0,1:T(4,128)} %param.19) | copy-start | bytes 1327108
  0.0 51.9 %collective-permute-start = (f32[4,12,2304]{2,0,1:T(4,128)}, f32[4,12,2304]{2,0,1:T(4,128)}, u32[]{:S(2)}, u32[]{:S(2)}) collective-permute-start(f32[4,12,2304]{2,0,1:T(4,128)} %param.19), channel_id=1, source_target_pairs={{0,4},{4,8},{8,12},{12,16},{16,20},{20,24},{24,28},{1,5},{5,9},{9,... | collective-permute-start | bytes 1327112 | tf_op jit(solution)/shard_map/ppermute | solution.py:20
  5.7 47.3 %collective-permute-start.1 = (f32[4,12,2304]{2,0,1:T(4,128)}, f32[4,12,2304]{2,0,1:T(4,128)}, u32[]{:S(2)}, u32[]{:S(2)}) collective-permute-start(f32[4,12,2304]{2,0,1:T(4,128)} %param.19), channel_id=1, source_target_pairs={{4,0},{8,4},{12,8},{16,12},{20,16},{24,20},{28,24},{5,1},{9,5},{13... | collective-permute-start | bytes 1327112 | tf_op jit(solution)/shard_map/ppermute | solution.py:20
  9.3 4.0 %copy-start.14 = (f32[2,6]{1,0:T(2,128)S(1)}, f32[2,6]{1,0:T(2,128)}, u32[]{:S(2)}) copy-start(f32[2,6]{1,0:T(2,128)} %param.26) | copy-start | bytes 148
  9.3 4.0 %copy-start.15 = (f32[6]{0:T(128)S(1)}, f32[6]{0:T(128)}, u32[]{:S(2)}) copy-start(f32[6]{0:T(128)} %param.27) | copy-start | bytes 76
  9.3 4.1 %copy-start.18 = (s32[4]{0:T(128)S(1)}, s32[4]{0:T(128)}, u32[]{:S(2)}) copy-start(s32[4]{0:T(128)} %param.23) | copy-start | bytes 52
  9.3 4.1 %copy-start.16 = (f32[4]{0:T(128)S(1)}, f32[4]{0:T(128)}, u32[]{:S(2)}) copy-start(f32[4]{0:T(128)} %param.29) | copy-start | bytes 52
  9.3 4.1 %copy-start.17 = (f32[4]{0:T(128)S(1)}, f32[4]{0:T(128)}, u32[]{:S(2)}) copy-start(f32[4]{0:T(128)} %param.28) | copy-start | bytes 52
  9.3 4.4 %copy-start.12 = (f32[2,4,4]{2,1,0:T(4,128)S(1)}, f32[2,4,4]{2,1,0:T(4,128)}, u32[]{:S(2)}) copy-start(f32[2,4,4]{2,1,0:T(4,128)} %param.25) | copy-start | bytes 388
  9.3 11.5 %all-to-all-start = ((f32[4,1,12,2304]{3,1,2,0:T(1,128)}), f32[4,1,12,2304]{3,1,2,0:T(1,128)S(1)}, u32[]{:S(2)}, u32[]{:S(2)}) async-start(f32[4,1,12,2304]{3,1,2,0:T(1,128)} %copy.57), calls=%async_computation | async-start | bytes 884736 | tf_op jit(solution)/shard_map/all_to_all | solution.py:340
  22.7 1.0 %copy-start.4 = (bf16[2,256,256]{2,1,0:T(8,128)(2,1)S(1)}, bf16[2,256,256]{2,1,0:T(8,128)(2,1)}, u32[]{:S(2)}) copy-start(bf16[2,256,256]{2,1,0:T(8,128)(2,1)} %constant.52.clone.iz_ref) | copy-start | bytes 786436
  22.7 1.0 %copy-start.5 = (bf16[2,128,256]{2,1,0:T(8,128)(2,1)S(1)}, bf16[2,128,256]{2,1,0:T(8,128)(2,1)}, u32[]{:S(2)}) copy-start(bf16[2,128,256]{2,1,0:T(8,128)(2,1)} %constant.50.clone.fz_ref) | copy-start | bytes 393220
  22.7 1.0 %copy-start.6 = (f32[3,48,128]{2,1,0:T(8,128)S(1)}, f32[3,48,128]{2,1,0:T(8,128)}, u32[]{:S(2)}) copy-start(f32[3,48,128]{2,1,0:T(8,128)} %constant.56.clone.vel_ref) | copy-start | bytes 221188
  22.7 1.0 %copy-start.7 = (bf16[96,144]{1,0:T(8,128)(2,1)S(1)}, bf16[96,144]{1,0:T(8,128)(2,1)}, u32[]{:S(2)}) copy-start(bf16[96,144]{1,0:T(8,128)(2,1)} %constant.51.clone.fyx_ref) | copy-start | bytes 82948
  22.7 1.0 %copy-start.8 = (bf16[48,144]{1,0:T(8,128)(2,1)S(1)}, bf16[48,144]{1,0:T(8,128)(2,1)}, u32[]{:S(2)}) copy-start(bf16[48,144]{1,0:T(8,128)(2,1)} %constant.53.clone.iv_ref) | copy-start | bytes 41476
  22.8 1.0 %copy-start.9 = (f32[48,128]{1,0:T(8,128)S(1)}, f32[48,128]{1,0:T(8,128)}, u32[]{:S(2)}) copy-start(f32[48,128]{1,0:T(8,128)} %constant.54.clone.freq_ref) | copy-start | bytes 73732
  22.8 1.0 %copy-start.10 = (f32[1,128]{1,0:T(1,128)S(1)}, f32[1,128]{1,0:T(1,128)}, u32[]{:S(2)}) copy-start(f32[1,128]{1,0:T(1,128)} %constant.55.clone.lane_ref) | copy-start | bytes 1540
  46.4 5.5 %copy-start.13 = (s32[4,4]{1,0:T(4,128)S(1)}, s32[4,4]{1,0:T(4,128)}, u32[]{:S(2)}) copy-start(s32[4,4]{1,0:T(4,128)} %param.21) | copy-start | bytes 196
  48.3 11.4 %all-to-all-start.1 = ((f32[1,1,48,2304]{3,1,0,2:T(1,128)}), f32[1,1,48,2304]{3,1,0,2:T(1,128)S(1)}, u32[]{:S(2)}, u32[]{:S(2)}) async-start(f32[1,1,48,2304]{3,1,0,2:T(1,128)} %reshape_stack_reshape.4), calls=%async_computation.1 | async-start | bytes 884736 | tf_op jit(solution)/shard_map/all_to_all | solution.py:357
  51.8 2.3 %copy-start = (f32[12,2304]{1,0:T(8,128)S(1)}, f32[12,2304]{1,0:T(8,128)}, u32[]{:S(2)}) copy-start(f32[12,2304]{1,0:T(8,128)} %inflow_ref.1) | copy-start | bytes 331780
  51.8 2.3 %copy-start.1 = (f32[2,2304]{1,0:T(2,128)S(1)}, f32[2,2304]{1,0:T(2,128)}, u32[]{:S(2)}) copy-start(f32[2,2304]{1,0:T(2,128)} %constant.49.clone.vel_ref) | copy-start | bytes 55300
  51.8 2.3 %copy-start.2 = (s32[4,4]{1,0:T(4,128)S(1)}, s32[4,4]{1,0:T(4,128)}, u32[]{:S(2)}) copy-start(s32[4,4]{1,0:T(4,128)} %kind_ref.1) | copy-start | bytes 196
  51.8 2.3 %copy-start.3 = (f32[4,4]{1,0:T(4,128)S(1)}, f32[4,4]{1,0:T(4,128)}, u32[]{:S(2)}) copy-start(f32[4,4]{1,0:T(4,128)} %coef_ref.1) | copy-start | bytes 196
